TPU v7x, 256 devices: a whole 4x4x8 slice. The times are simulated.
256 devices in a mesh: pair: 32 (over y, x, core), grow: 4 (over z_hi), gcol: 2 (over z_lo).
Axes of the slice: x: 4, y: 4, z: 8 (z_hi: 4, z_lo: 2; z = z_hi * 2 + z_lo), core: 2. Of those that a mesh axis runs over, the one named last changes fastest.
Arguments:
- slab_density: bfloat16 [8192, 16], P('pair', ('grow', 'gcol')), may hold values from -0.62890625 to 0.62890625
- column_density: bfloat16 [8192, 12288], P('pair', ('gcol', 'grow')), may hold values from -0.62890625 to 0.62890625
- bin_index: int32 [8192], P('pair'), may hold values from 0 to 127
- occupation: int32 [8192], P('pair'), may hold values from -1 to 1, as said below
Outputs:
- polarization: float32 [64, 16, 12288], P(None, 'grow', ('gcol', 'pair'))
Inputs may be any that keep to these rules, and one draw needn't show every extreme that they name: `occupation`: each entry is -1 or +1.
All inputs are finite; a program needn't handle non-finite values.
Results may differ from a plain program's by a relative error of at most 0.0003.
Values may be sent and summed in bfloat16 or wider, within the bound.
No kernel may reach another device: no remote copies, remote signals or barrier semaphores. Data moves between devices by JAX's collectives and lax.ppermute only.
A program may use at most 64 MiB of HBM per device.

v0:
```python
import jax
import jax.numpy as jnp
from jax import lax
from jax.sharding import PartitionSpec as P

BINS = 128
FREQS = 64


def hilbert_table():
    energies = (jnp.arange(BINS, dtype=jnp.float32) + 0.5) * (4.0 / BINS)
    real_freq = (jnp.arange(FREQS, dtype=jnp.float32) + 0.5) * (4.0 / FREQS)
    broadening = 4.0 / BINS
    below = real_freq[:, None] - energies[None, :]
    above = real_freq[:, None] + energies[None, :]
    return below / (below * below + broadening * broadening) - above / (
        above * above + broadening * broadening
    )


def per_device(slab_density, column_density, bin_index, occupation):
    slab_rows = lax.all_gather(slab_density, "gcol", axis=1, tiled=True)
    pair_count = slab_rows.shape[0]
    row_count = slab_rows.shape[1]
    kernel = hilbert_table()
    occupied = (bin_index[:, None] == jnp.arange(BINS, dtype=jnp.int32)[None, :]).astype(
        jnp.float32
    )
    occupied = occupied * occupation[:, None].astype(jnp.float32)
    pair_weight = jnp.dot(occupied, kernel.T, precision=lax.Precision.HIGHEST)
    weighted_left = (pair_weight[:, :, None] * slab_rows.astype(jnp.float32)[:, None, :]).reshape(
        pair_count, FREQS * row_count
    )
    leading = FREQS
    partial_sums = lax.dot_general(
        weighted_left,
        lax.all_gather(column_density, "grow", axis=1, tiled=True).astype(jnp.float32),
        (((0,), (0,)), ((), ())),
        precision=lax.Precision.HIGHEST,
    )
    tiles = partial_sums.reshape(leading, row_count, partial_sums.shape[1])
    polarization = lax.psum_scatter(tiles, "pair", scatter_dimension=2, tiled=True)
    return polarization


def solution(mesh):
    placed = (P("pair", ("grow", "gcol")), P("pair", ("gcol", "grow")), P("pair"), P("pair"))
    return jax.shard_map(
        per_device,
        mesh=mesh,
        in_specs=placed,
        out_specs=P(None, "grow", ("gcol", "pair")),
        check_vma=False,
    )
```

profile of v0, /device:TPU:17, one launch (start us, length us, event | category | flops | bytes accessed | tf_op | source)
XLA Modules:
  0.0 210.2 jit_solution(13664309245588123736)
XLA Ops:
  6.5 0.0 all-gather.3.cloned.1.call-start
  6.5 0.7 all-gather.3.cloned.1.call-update
  7.3 0.0 reduce-scatter.4.cloned.1.call-start
  7.3 0.7 convert_element_type.9
  8.0 3.5 %all-gather = bf16[2,2,256]{2,1,0:T(2,128)(2,1)S(1)} all-gather(bf16[1,2,256]{2,1,0:T(2,128)(2,1)} %bitcast.17), channel_id=1, replica_groups=mesh['pair'=32,'grow'=4,'gcol'=2] {'gcol'}, dimensions={0}, use_global_device_ids=true | all-gather | bytes 3072 | tf_op jit(solution)/shard_map/all_gather | solution.py:22
  11.5 1.0 fusion.3
  12.6 0.1 mul.62
  12.7 0.1 dot_general.12
  12.8 68.1 %all-gather.3.cloned.1.call-done = bf16[256,6144]{1,0:T(8,128)(2,1)} async-done(((bf16[256,1536]{1,0:T(8,128)(2,1)}), bf16[256,6144]{1,0:T(8,128)(2,1)}) %all-gather.3.cloned.1.call-update) | async-done | bytes 3145744 | tf_op jit(solution)/shard_map/all_gather | solution.py:37
  80.9 6.4 %fusion = f32[64,4,6144]{2,0,1:T(8,128)} fusion(bf16[256,6144]{1,0:T(8,128)(2,1)} %all-gather.3.cloned.1.call-done, f32[64,4,256]{2,1,0:T(4,128)S(1)} %dot_general.12), kind=kOutput, calls=%fused_computation | convolution fusion | flops 4831838208 | bytes 9699328 | tf_op jit(solution)/shard_map/dot_general | solution.py:35
  87.2 11.9 %copy.12 = f32[64,4,6144]{0,1,2:T(4,128)} copy(f32[64,4,6144]{2,0,1:T(8,128)} %fusion) | data formatting | bytes 12582912
  99.1 12.4 %reshape.25 = f32[6144,256]{1,0:T(8,128)} reshape(f32[6144,4,64]{2,1,0:T(4,128)} %bitcast.13) | data formatting | bytes 12582912
  111.5 0.0 reduce-scatter.4.cloned.1.call-update
  111.6 89.7 %reduce-scatter.4.cloned.1.call-done = f32[192,256]{1,0:T(8,128)} async-done(((f32[6144,256]{1,0:T(8,128)}), f32[192,256]{1,0:T(8,128)}) %reduce-scatter.4.cloned.1.call-update) | async-done | bytes 196624
  201.3 1.1 reshape.26
  202.4 0.9 copy.11
  (4 shorter events, 0.1 us)
Async XLA Ops:
  6.5 74.3 %all-gather.3.cloned.1.call-start = ((), (), s32[]{:S(2)}) async-start(), calls=%async_computation.1 | async-start | bytes 3932160 | tf_op jit(solution)/shard_map/all_gather | solution.py:37
  7.3 194.0 %reduce-scatter.4.cloned.1.call-start = ((), (), s32[]{:S(2)}) async-start(), calls=%async_computation.2 | async-start | bytes 6488064
Sparse Core Ops, SparseCore 0:
  9.2 71.6 all-gather.2
  111.7 89.5 reduce-scatter.3
where the time goes:
time: 213 us; the launch traced here: 210 us
  waiting for transfers between devices  159 us (75%)
  local copies, waits for them, and re-layouts  26.5 us (12%)
  between operations  13.4 us (6%)
  matrix products  7.41 us (3%)
  blocking collectives  3.51 us (2%)
    unnamed x3, waiting for transfers between devices  90.5 us
    all_gather x1, waiting for transfers between devices, per_device(): lax.all_gather(column_density, 'grow', axis=1, tiled=True)  68.1 us
    unnamed x3, local copies, waits for them, and re-layouts  25.4 us
    dot_general x1, matrix products, per_device(): lax.dot_general(weighted_left, lax.all_gather(column_density, 'grow', axi...  6.36 us
  transfers between devices with their start and end apart: 2, of which 2 were waited for; matrix products, arithmetic and copies ran while one was open for 1% of the time, Pallas kernels for 0%

commit v1 on v0

v1 whole, which is shorter than its diff:
```python
import functools

import jax
import jax.numpy as jnp
import numpy as np
from jax import lax
from jax.experimental import pallas as pl
from jax.experimental.pallas import tpu as pltpu
from jax.sharding import PartitionSpec as P

BINS = 128
FREQS = 64
GR = 16
Y = 4
X = 4
CORES = 2
Z = 4
CHIPS = Y * X
PART = 48
BF16 = jnp.bfloat16


def hilbert_table():
    one = np.float32
    energies = (np.arange(BINS, dtype=np.float32) + one(0.5)) * one(4.0 / BINS)
    real_freq = (np.arange(FREQS, dtype=np.float32) + one(0.5)) * one(4.0 / FREQS)
    broadening = one(4.0 / BINS)
    below = real_freq[:, None] - energies[None, :]
    above = real_freq[:, None] + energies[None, :]
    return below / (below * below + broadening * broadening) - above / (
        above * above + broadening * broadening
    )


def place(y, xc, z):
    return (y * X * CORES + xc) * Z + z


def polarize(table_ref, recv_ref, out_ref, hot_ref):
    pairs = recv_ref.shape[2]
    cols = CORES * PART
    bin_of_row = lax.broadcasted_iota(jnp.int32, (BINS, pairs), 0).astype(jnp.float32)
    for source in range(CHIPS):
        bins = recv_ref[source, cols + GR : cols + 2 * GR, :].astype(jnp.float32)[0:1, :]
        hot_ref[source] = jnp.where(bins == bin_of_row, 1.0, 0.0).astype(BF16)
    table = table_ref[...]
    for group in range(Z):
        total = jnp.zeros((4 * BINS, cols), jnp.float32)
        for source in range(CHIPS):
            hot = hot_ref[source]
            slab = recv_ref[source, cols : cols + GR, :]
            left = jnp.concatenate(
                [hot * slab[4 * group + i : 4 * group + i + 1, :] for i in range(4)], axis=0
            )
            total = total + lax.dot_general(
                left,
                recv_ref[source, :cols, :],
                (((1,), (1,)), ((), ())),
                preferred_element_type=jnp.float32,
            )
        for half in range(2):
            both = [
                jnp.dot(
                    table,
                    total[(2 * half + i) * BINS : (2 * half + i + 1) * BINS, :],
                    precision=lax.Precision.HIGHEST,
                    preferred_element_type=jnp.float32,
                )
                for i in range(2)
            ]
            lane = (2 * group + half) * 2 * FREQS
            out_ref[:, lane : lane + 2 * FREQS] = jnp.concatenate(both, axis=0).T


def per_device(slab_density, column_density, bin_index, occupation):
    pairs = slab_density.shape[0]
    me = lax.axis_index("pair")
    core = me % CORES
    my_y = me // (X * CORES)
    my_z = lax.axis_index("grow")

    signed = (slab_density * occupation[:, None].astype(BF16)).T
    rows = jnp.concatenate(
        [signed, lax.ppermute(signed, "gcol", [(0, 1), (1, 0)])], axis=0
    )
    gcol = lax.axis_index("gcol")
    rows = jnp.where(gcol == 0, rows, jnp.roll(rows, 2, axis=0))
    slabs = jnp.zeros((Z, 4, pairs), BF16)
    slabs = lax.dynamic_update_index_in_dim(slabs, rows, my_z, 0)
    for t in range(1, Z):
        got = lax.ppermute(rows, "grow", [(z, (z + t) % Z) for z in range(Z)])
        slabs = lax.dynamic_update_index_in_dim(slabs, got, (my_z - t) % Z, 0)
    meta = jnp.concatenate(
        [
            slabs.reshape(GR, pairs),
            jnp.broadcast_to(bin_index.astype(BF16)[None, :], (GR, pairs)),
        ],
        axis=0,
    )

    columns = column_density.T.reshape(X, CORES, Y, PART, pairs)
    columns = columns.transpose(2, 0, 1, 3, 4).reshape(CHIPS, CORES * PART, pairs)
    payload = jnp.concatenate(
        [columns, jnp.broadcast_to(meta[None], (CHIPS, 2 * GR, pairs))], axis=1
    )
    groups = [
        [(y * X + x) * CORES + c for y in range(Y) for x in range(X)] for c in range(CORES)
    ]
    received = lax.all_to_all(
        payload, "pair", 0, 0, axis_index_groups=groups, tiled=True
    )

    lanes = GR * FREQS
    part = pl.pallas_call(
        polarize,
        out_shape=jax.ShapeDtypeStruct((CORES * PART, lanes), jnp.float32),
        scratch_shapes=[pltpu.VMEM((CHIPS, BINS, pairs), BF16)],
        compiler_params=pltpu.CompilerParams(vmem_limit_bytes=40 * 1024 * 1024),
    )(jnp.asarray(hilbert_table()), received)

    part = part.reshape(CORES, PART, lanes)
    mine = lax.dynamic_index_in_dim(part, core, 0, keepdims=False)
    other = lax.dynamic_index_in_dim(part, 1 - core, 0, keepdims=False)
    swap = [(i, i ^ 1) for i in range(Y * X * CORES)]
    summed = mine + lax.ppermute(other, "pair", swap)

    width = 4 * FREQS
    tiles = jnp.zeros((Y, PART, width), jnp.float32)
    for t in range(Z):
        piece = lax.dynamic_slice_in_dim(summed, (my_y + t) % Z * width, width, 1)
        got = lax.ppermute(
            piece,
            ("pair", "grow"),
            [
                (place(y, xc, z), place(z, xc, (y + t) % Z))
                for y in range(Y)
                for xc in range(X * CORES)
                for z in range(Z)
            ],
        )
        tiles = lax.dynamic_update_index_in_dim(tiles, got, (my_z - t) % Z, 0)
    return tiles.reshape(Y * PART, 4, FREQS).transpose(2, 1, 0)


def solution(mesh):
    placed = (P("pair", ("grow", "gcol")), P("pair", ("gcol", "grow")), P("pair"), P("pair"))
    return jax.shard_map(
        per_device,
        mesh=mesh,
        in_specs=placed,
        out_specs=P(None, "grow", ("gcol", "pair")),
        check_vma=False,
    )
```

time: 213 us -> 72.6 us (0.34)
  the two profiles are of different devices: /device:TPU:17 before, /device:TPU:8 now
where the time goes in v1:
time: 72.6 us; the launch traced here: 72.3 us
  starting transfers between devices  35.1 us (48%)
  waiting for transfers between devices  20.9 us (29%)
  Pallas kernels  10.1 us (14%)
  other arithmetic  3.15 us (4%)
  local copies, waits for them, and re-layouts  2.75 us (4%)
    ppermute x4, starting transfers between devices, per_device(): lax.ppermute(piece, ('pair', 'grow'), [(place(y, xc, z), place(z, xc, (y...  14.7 us
    all_to_all x1, waiting for transfers between devices, per_device(): lax.all_to_all(payload, 'pair', 0, 0, axis_index_groups=groups, tiled=True)  12.9 us
    ppermute x3, starting transfers between devices, per_device(): got = lax.ppermute(rows, 'grow', [(z, (z + t) % Z) for z in range(Z)])  10.8 us
    pallas_call x1, Pallas kernels, per_device(): pl.pallas_call(polarize, out_shape=jax.ShapeDtypeStruct((CORES * PART, la...  10.1 us
    all_to_all x1, starting transfers between devices, per_device(): lax.all_to_all(payload, 'pair', 0, 0, axis_index_groups=groups, tiled=True)  7.52 us
    ppermute x4, waiting for transfers between devices, per_device(): lax.ppermute(piece, ('pair', 'grow'), [(place(y, xc, z), place(z, xc, (y...  4.94 us
    ppermute x1, starting transfers between devices, per_device(): lax.ppermute(signed, 'gcol', [(0, 1), (1, 0)])  1.92 us
    ppermute x3, waiting for transfers between devices, per_device(): got = lax.ppermute(rows, 'grow', [(z, (z + t) % Z) for z in range(Z)])  1.75 us
  transfers between devices with their start and end apart: 10, of which 6 were waited for; matrix products, arithmetic and copies ran while one was open for 3% of the time, Pallas kernels for 0%

profile of v1, /device:TPU:8, one launch (start us, length us, event | category | flops | bytes accessed | tf_op | source)
XLA Modules:
  0.0 72.3 jit_solution(15083106969278493951)
XLA Ops:
  0.0 0.7 convert_element_type.7
  0.7 0.7 multiply_bitcast_fusion
  1.4 1.9 %collective-permute-start = (bf16[2,256]{1,0:T(2,128)(2,1)S(1)}, bf16[2,256]{1,0:T(2,128)(2,1)S(1)}, u32[]{:S(2)}, u32[]{:S(2)}) collective-permute-start(bf16[2,256]{1,0:T(2,128)(2,1)S(1)} %get-tuple-element.10), channel_id=1, source_target_pairs={{0,1},{1,0},{2,3},{3,2},{4,5},{5,4},{6,7},{7,6},{8,9},{9,8},{10,11... | collective-permute-start | bytes 3080 | tf_op jit(solution)/shard_map/ppermute | solution.py:84
  3.3 0.7 convert_element_type.8
  4.0 1.4 %copy.7 = bf16[256,1536]{0,1:T(8,128)(2,1)S(1)} copy(bf16[256,1536]{1,0:T(8,128)(2,1)} %param.6) | data formatting | bytes 1572864 | tf_op args[1]
  5.4 0.1 copy.8
  5.5 0.0 collective-permute-done
  5.5 3.3 %collective-permute-start.1 = (bf16[4,256]{1,0:T(4,128)(2,1)S(1)}, bf16[4,256]{1,0:T(4,128)(2,1)S(1)}, u32[]{:S(2)}, u32[]{:S(2)}) collective-permute-start(bf16[4,256]{1,0:T(4,128)(2,1)S(1)} %maximum_select_fusion.1), channel_id=1, source_target_pairs={{0,2},{2,4},{4,6},{6,0},{1,3},{3,5},{5,7},{7,1},{8,10},{10,12},{12... | collective-permute-start | bytes 6152 | tf_op jit(solution)/shard_map/ppermute | solution.py:91
  8.9 4.8 %collective-permute-start.2 = (bf16[4,256]{1,0:T(4,128)(2,1)S(1)}, bf16[4,256]{1,0:T(4,128)(2,1)S(1)}, u32[]{:S(2)}, u32[]{:S(2)}) collective-permute-start(bf16[4,256]{1,0:T(4,128)(2,1)S(1)} %maximum_select_fusion.1), channel_id=1, source_target_pairs={{0,4},{2,6},{4,0},{6,2},{1,5},{3,7},{5,1},{7,3},{8,12},{10,14},{12... | collective-permute-start | bytes 6152 | tf_op jit(solution)/shard_map/ppermute | solution.py:91
  13.7 2.7 %collective-permute-start.3 = (bf16[4,256]{1,0:T(4,128)(2,1)S(1)}, bf16[4,256]{1,0:T(4,128)(2,1)S(1)}, u32[]{:S(2)}, u32[]{:S(2)}) collective-permute-start(bf16[4,256]{1,0:T(4,128)(2,1)S(1)} %maximum_select_fusion.1), channel_id=1, source_target_pairs={{0,6},{2,0},{4,2},{6,4},{1,7},{3,1},{5,3},{7,5},{8,14},{10,8},{12,... | collective-permute-start | bytes 6152 | tf_op jit(solution)/shard_map/ppermute | solution.py:91
  16.4 0.0 collective-permute-done.1
  16.4 0.0 collective-permute-done.2
  16.4 1.7 %collective-permute-done.3 = bf16[4,256]{1,0:T(4,128)(2,1)S(1)} collective-permute-done((bf16[4,256]{1,0:T(4,128)(2,1)S(1)}, bf16[4,256]{1,0:T(4,128)(2,1)S(1)}, u32[]{:S(2)}, u32[]{:S(2)}) %collective-permute-start.3) | collective-permute-done | bytes 2080 | tf_op jit(solution)/shard_map/ppermute | solution.py:91
  18.2 1.0 %pad_maximum_fusion = bf16[16,128,256]{2,1,0:T(8,128)(2,1)} fusion(bf16[16,32,256]{2,1,0:T(8,128)(2,1)S(1)} %broadcast_in_dim.49, bf16[16,96,256]{2,1,0:T(8,128)(2,1)S(1)} %bitcast.35), kind=kLoop, calls=%fused_computation | loop fusion | flops 2097152 | bytes 2097152 | tf_op jit(solution)/shard_map/concatenate | solution.py:103
  19.3 0.0 copy-start
  19.3 7.5 %all-to-all-start = ((bf16[16,128,256]{2,1,0:T(8,128)(2,1)}), bf16[16,128,256]{2,1,0:T(8,128)(2,1)S(1)}, u32[]{:S(2)}, u32[]{:S(2)}) async-start(bf16[16,128,256]{2,1,0:T(8,128)(2,1)} %pad_maximum_fusion), calls=%async_computation | async-start | bytes 2097152 | tf_op jit(solution)/shard_map/all_to_all | solution.py:109
  26.8 12.9 %all-to-all-done.recv_ref = bf16[16,128,256]{2,1,0:T(8,128)(2,1)S(1)} async-done(((bf16[16,128,256]{2,1,0:T(8,128)(2,1)}), bf16[16,128,256]{2,1,0:T(8,128)(2,1)S(1)}, u32[]{:S(2)}, u32[]{:S(2)}) %all-to-all-start) | async-done | bytes 1048608 | tf_op jit(solution)/shard_map/all_to_all | solution.py:109
  39.7 0.0 copy-done
  39.7 10.1 %shard_map.55 = f32[96,1024]{1,0:T(8,128)S(1)} custom-call(f32[64,128]{1,0:T(8,128)S(1)} %copy-done, bf16[16,128,256]{2,1,0:T(8,128)(2,1)S(1)} %all-to-all-done.recv_ref), custom_call_target="tpu_custom_call" | custom-call | tf_op jit(solution)/shard_map/pallas_call | solution.py:114
  49.9 0.1 collective-permute-start.4
  50.1 1.3 %collective-permute-done.4 = f32[48,1024]{1,0:T(8,128)S(1)} collective-permute-done((f32[48,1024]{1,0:T(8,128)S(1)}, f32[48,1024]{1,0:T(8,128)S(1)}, u32[]{:S(2)}, u32[]{:S(2)}) %collective-permute-start.4) | collective-permute-done | bytes 196640 | tf_op jit(solution)/shard_map/ppermute | solution.py:125
  51.5 6.2 %collective-permute-start.5 = (f32[48,256]{1,0:T(8,128)S(1)}, f32[48,256]{1,0:T(8,128)S(1)}, u32[]{:S(2)}, u32[]{:S(2)}) collective-permute-start(f32[48,256]{1,0:T(8,128)S(1)} %get-tuple-element.8), channel_id=1, source_target_pairs={{0,0},{2,64},{4,128},{6,192},{8,8},{10,72},{12,136},{14,200},{16,1... | collective-permute-start | bytes 147464 | tf_op jit(solution)/shard_map/ppermute | solution.py:131
  57.7 4.2 %collective-permute-start.6 = (f32[48,256]{1,0:T(8,128)S(1)}, f32[48,256]{1,0:T(8,128)S(1)}, u32[]{:S(2)}, u32[]{:S(2)}) collective-permute-start(f32[48,256]{1,0:T(8,128)S(1)} %get-tuple-element.7), channel_id=1, source_target_pairs={{0,2},{2,66},{4,130},{6,194},{8,10},{10,74},{12,138},{14,202},{16,... | collective-permute-start | bytes 147464 | tf_op jit(solution)/shard_map/ppermute | solution.py:131
  61.9 4.3 %collective-permute-start.7 = (f32[48,256]{1,0:T(8,128)S(1)}, f32[48,256]{1,0:T(8,128)S(1)}, u32[]{:S(2)}, u32[]{:S(2)}) collective-permute-start(f32[48,256]{1,0:T(8,128)S(1)} %get-tuple-element.6), channel_id=1, source_target_pairs={{0,4},{2,68},{4,132},{6,196},{8,12},{10,76},{12,140},{14,204},{16,... | collective-permute-start | bytes 147464 | tf_op jit(solution)/shard_map/ppermute | solution.py:131
  66.2 0.0 collective-permute-start.8
  66.2 0.0 collective-permute-done.5
  66.2 0.4 collective-permute-done.6
  66.6 2.9 %collective-permute-done.7 = f32[48,256]{1,0:T(8,128)S(1)} collective-permute-done((f32[48,256]{1,0:T(8,128)S(1)}, f32[48,256]{1,0:T(8,128)S(1)}, u32[]{:S(2)}, u32[]{:S(2)}) %collective-permute-start.7) | collective-permute-done | bytes 49184 | tf_op jit(solution)/shard_map/ppermute | solution.py:131
  69.5 1.6 %collective-permute-done.8 = f32[48,256]{1,0:T(8,128)S(1)} collective-permute-done((f32[48,256]{1,0:T(8,128)S(1)}, f32[48,256]{1,0:T(8,128)S(1)}, u32[]{:S(2)}, u32[]{:S(2)}) %collective-permute-start.8) | collective-permute-done | bytes 49184 | tf_op jit(solution)/shard_map/ppermute | solution.py:131
  71.2 0.2 reshape.78
  71.4 0.9 %copy.9 = f32[64,4,192]{2,1,0:T(4,128)} copy(f32[64,4,192]{0,1,2:T(4,128)S(1)} %bitcast.36) | data formatting | bytes 393216 | tf_op jit(solution)/shard_map/transpose | solution.py:142
  (18 shorter events, 0.2 us)
Async XLA Ops:
  1.4 4.1 %collective-permute-start = (bf16[2,256]{1,0:T(2,128)(2,1)S(1)}, bf16[2,256]{1,0:T(2,128)(2,1)S(1)}, u32[]{:S(2)}, u32[]{:S(2)}) collective-permute-start(bf16[2,256]{1,0:T(2,128)(2,1)S(1)} %get-tuple-element.10), channel_id=1, source_target_pairs={{0,1},{1,0},{2,3},{3,2},{4,5},{5,4},{6,7},{7,6},{8,9},{9,8},{10,11... | collective-permute-start | bytes 3080 | tf_op jit(solution)/shard_map/ppermute | solution.py:84
  5.5 10.9 %collective-permute-start.1 = (bf16[4,256]{1,0:T(4,128)(2,1)S(1)}, bf16[4,256]{1,0:T(4,128)(2,1)S(1)}, u32[]{:S(2)}, u32[]{:S(2)}) collective-permute-start(bf16[4,256]{1,0:T(4,128)(2,1)S(1)} %maximum_select_fusion.1), channel_id=1, source_target_pairs={{0,2},{2,4},{4,6},{6,0},{1,3},{3,5},{5,7},{7,1},{8,10},{10,12},{12... | collective-permute-start | bytes 6152 | tf_op jit(solution)/shard_map/ppermute | solution.py:91
  8.9 7.5 %collective-permute-start.2 = (bf16[4,256]{1,0:T(4,128)(2,1)S(1)}, bf16[4,256]{1,0:T(4,128)(2,1)S(1)}, u32[]{:S(2)}, u32[]{:S(2)}) collective-permute-start(bf16[4,256]{1,0:T(4,128)(2,1)S(1)} %maximum_select_fusion.1), channel_id=1, source_target_pairs={{0,4},{2,6},{4,0},{6,2},{1,5},{3,7},{5,1},{7,3},{8,12},{10,14},{12... | collective-permute-start | bytes 6152 | tf_op jit(solution)/shard_map/ppermute | solution.py:91
  13.7 4.5 %collective-permute-start.3 = (bf16[4,256]{1,0:T(4,128)(2,1)S(1)}, bf16[4,256]{1,0:T(4,128)(2,1)S(1)}, u32[]{:S(2)}, u32[]{:S(2)}) collective-permute-start(bf16[4,256]{1,0:T(4,128)(2,1)S(1)} %maximum_select_fusion.1), channel_id=1, source_target_pairs={{0,6},{2,0},{4,2},{6,4},{1,7},{3,1},{5,3},{7,5},{8,14},{10,8},{12,... | collective-permute-start | bytes 6152 | tf_op jit(solution)/shard_map/ppermute | solution.py:91
  19.3 20.4 %copy-start = (f32[64,128]{1,0:T(8,128)S(1)}, f32[64,128]{1,0:T(8,128)}, u32[]{:S(2)}) copy-start(f32[64,128]{1,0:T(8,128)} %constant.128.clone.table_ref) | copy-start | bytes 98308
  19.3 20.4 %all-to-all-start = ((bf16[16,128,256]{2,1,0:T(8,128)(2,1)}), bf16[16,128,256]{2,1,0:T(8,128)(2,1)S(1)}, u32[]{:S(2)}, u32[]{:S(2)}) async-start(bf16[16,128,256]{2,1,0:T(8,128)(2,1)} %pad_maximum_fusion), calls=%async_computation | async-start | bytes 2097152 | tf_op jit(solution)/shard_map/all_to_all | solution.py:109
  49.9 1.5 %collective-permute-start.4 = (f32[48,1024]{1,0:T(8,128)S(1)}, f32[48,1024]{1,0:T(8,128)S(1)}, u32[]{:S(2)}, u32[]{:S(2)}) collective-permute-start(f32[48,1024]{1,0:T(8,128)S(1)} %dynamic-slice_bitcast_fusion), channel_id=1, source_target_pairs={{0,8},{8,0},{16,24},{24,16},{32,40},{40,32},{48,56},{56,48},{64,72... | collective-permute-start | bytes 589832 | tf_op jit(solution)/shard_map/ppermute | solution.py:125
  51.5 14.7 %collective-permute-start.5 = (f32[48,256]{1,0:T(8,128)S(1)}, f32[48,256]{1,0:T(8,128)S(1)}, u32[]{:S(2)}, u32[]{:S(2)}) collective-permute-start(f32[48,256]{1,0:T(8,128)S(1)} %get-tuple-element.8), channel_id=1, source_target_pairs={{0,0},{2,64},{4,128},{6,192},{8,8},{10,72},{12,136},{14,200},{16,1... | collective-permute-start | bytes 147464 | tf_op jit(solution)/shard_map/ppermute | solution.py:131
  57.7 8.9 %collective-permute-start.6 = (f32[48,256]{1,0:T(8,128)S(1)}, f32[48,256]{1,0:T(8,128)S(1)}, u32[]{:S(2)}, u32[]{:S(2)}) collective-permute-start(f32[48,256]{1,0:T(8,128)S(1)} %get-tuple-element.7), channel_id=1, source_target_pairs={{0,2},{2,66},{4,130},{6,194},{8,10},{10,74},{12,138},{14,202},{16,... | collective-permute-start | bytes 147464 | tf_op jit(solution)/shard_map/ppermute | solution.py:131
  61.9 7.7 %collective-permute-start.7 = (f32[48,256]{1,0:T(8,128)S(1)}, f32[48,256]{1,0:T(8,128)S(1)}, u32[]{:S(2)}, u32[]{:S(2)}) collective-permute-start(f32[48,256]{1,0:T(8,128)S(1)} %get-tuple-element.6), channel_id=1, source_target_pairs={{0,4},{2,68},{4,132},{6,196},{8,12},{10,76},{12,140},{14,204},{16,... | collective-permute-start | bytes 147464 | tf_op jit(solution)/shard_map/ppermute | solution.py:131
  66.2 5.0 %collective-permute-start.8 = (f32[48,256]{1,0:T(8,128)S(1)}, f32[48,256]{1,0:T(8,128)S(1)}, u32[]{:S(2)}, u32[]{:S(2)}) collective-permute-start(f32[48,256]{1,0:T(8,128)S(1)} %get-tuple-element.5), channel_id=1, source_target_pairs={{0,6},{2,70},{4,134},{6,198},{8,14},{10,78},{12,142},{14,206},{16,... | collective-permute-start | bytes 147464 | tf_op jit(solution)/shard_map/ppermute | solution.py:131

commit v2 on v0

v2 whole, which is shorter than its diff:
```python
import functools

import jax
import jax.numpy as jnp
import numpy as np
from jax import lax
from jax.experimental import pallas as pl
from jax.experimental.pallas import tpu as pltpu
from jax.sharding import PartitionSpec as P

BINS = 128
FREQS = 64
GR = 16
Y = 4
X = 4
CORES = 2
Z = 4
CHIPS = Y * X
PART = 48
COLS = CORES * PART
META = GR + 8
STEP = 4
BF16 = jnp.bfloat16
F32 = jnp.float32


def hilbert_table():
    energies = (np.arange(BINS, dtype=np.float32) + np.float32(0.5)) * np.float32(4.0 / BINS)
    real_freq = (np.arange(FREQS, dtype=np.float32) + np.float32(0.5)) * np.float32(4.0 / FREQS)
    broadening = np.float32(4.0 / BINS)
    below = real_freq[:, None] - energies[None, :]
    above = real_freq[:, None] + energies[None, :]
    return below / (below * below + broadening * broadening) - above / (
        above * above + broadening * broadening
    )


def split_table():
    table = hilbert_table()
    high = table.astype(jnp.bfloat16)
    low = (table - high.astype(np.float32)).astype(jnp.bfloat16)
    return np.block([[high, high], [low, low]])


def polarize(groups, table_ref, recv_ref, out_ref, sums_ref):
    pairs = recv_ref.shape[2]
    bin_of_row = lax.broadcasted_iota(jnp.int32, (BINS, pairs), 0).astype(F32)
    for first in range(0, CHIPS, STEP):
        hots = []
        for source in range(first, first + STEP):
            bins = recv_ref[source, COLS + GR : COLS + META, :].astype(F32)[0:1, :]
            hots.append(jnp.where(bins == bin_of_row, 1.0, 0.0).astype(BF16))
        for place, group in enumerate(groups):
            total = None
            for source, hot in enumerate(hots, first):
                slab = recv_ref[source, COLS : COLS + GR, :]
                left = jnp.concatenate(
                    [hot * slab[row : row + 1, :] for row in range(4 * group, 4 * group + 4)],
                    axis=0,
                )
                term = lax.dot_general(
                    left,
                    recv_ref[source, :COLS, :],
                    (((1,), (1,)), ((), ())),
                    preferred_element_type=F32,
                )
                total = term if total is None else total + term
            rows = slice(place * 4 * BINS, (place + 1) * 4 * BINS)
            if first == 0:
                sums_ref[rows, :] = total
            else:
                sums_ref[rows, :] += total
    table = table_ref[...]
    for duo in range(2 * len(groups)):
        both = []
        for row in (2 * duo, 2 * duo + 1):
            spectral = sums_ref[row * BINS : (row + 1) * BINS, :]
            high = spectral.astype(BF16)
            low = (spectral - high.astype(F32)).astype(BF16)
            out = jnp.dot(
                table, jnp.concatenate([high, low], axis=0), preferred_element_type=F32
            )
            both.append(out[:FREQS] + out[FREQS:])
        lane = duo % 2 * 2 * FREQS
        out_ref[duo // 2, :, lane : lane + 2 * FREQS] = jnp.concatenate(both, axis=0).T


def polarize_groups(groups, received):
    rows = len(groups) * 4 * BINS
    return pl.pallas_call(
        functools.partial(polarize, groups),
        out_shape=jax.ShapeDtypeStruct((len(groups), COLS, 4 * FREQS), F32),
        scratch_shapes=[pltpu.VMEM((rows, COLS), F32)],
        compiler_params=pltpu.CompilerParams(vmem_limit_bytes=40 * 1024 * 1024),
        cost_estimate=pl.CostEstimate(
            flops=2 * rows * COLS * received.shape[0] * received.shape[2],
            bytes_accessed=2 * received.size,
            transcendentals=0,
        ),
    )(jnp.asarray(split_table()), received)


def per_device(slab_density, column_density, bin_index, occupation):
    pairs = slab_density.shape[0]
    me = lax.axis_index("pair")
    core = me % CORES
    my_z = lax.axis_index("grow")

    signed = (slab_density * occupation[:, None].astype(BF16)).T
    slabs = lax.all_to_all(
        jnp.broadcast_to(signed[None], (GR // 2, 2, pairs)), ("grow", "gcol"), 0, 0, tiled=True
    ).reshape(Z, 4, pairs)

    twice = jnp.concatenate([slabs, slabs, slabs], axis=0)
    turned = jnp.stack(
        [lax.dynamic_slice_in_dim(twice, y + 2 * core, Z, 0) for y in range(Y)]
    ).reshape(Y, GR, pairs)
    bins = jnp.broadcast_to(bin_index.astype(BF16)[None, None, :], (Y, META - GR, pairs))
    meta = jnp.concatenate([turned, bins], axis=1)
    meta = jnp.broadcast_to(meta[:, None], (Y, X, META, pairs)).reshape(CHIPS, META, pairs)

    columns = column_density.T.reshape(X, CORES, Y, PART, pairs)
    columns = columns.transpose(2, 0, 1, 3, 4).reshape(CHIPS, COLS, pairs)
    received = lax.all_to_all(
        jnp.concatenate([columns, meta], axis=1),
        "pair",
        0,
        0,
        axis_index_groups=[
            [(y * X + x) * CORES + c for y in range(Y) for x in range(X)] for c in range(CORES)
        ],
        tiled=True,
    )

    swap = [(i, i ^ 1) for i in range(Y * X * CORES)]
    theirs = lax.ppermute(polarize_groups((2, 3), received), "pair", swap)
    summed = polarize_groups((0, 1), received) + theirs

    arrived = []
    for t in range(2):
        arrived.append(
            lax.ppermute(
                summed[t],
                ("pair", "grow"),
                [
                    (
                        ((y * X + x) * CORES + c) * Z + z,
                        ((z * X + x) * CORES + c) * Z + (y + 2 * c + t) % Z,
                    )
                    for y in range(Y)
                    for x in range(X)
                    for c in range(CORES)
                    for z in range(Z)
                ],
            )
        )
    arrived = jnp.stack(arrived).reshape(2, CORES, PART, 4 * FREQS)
    keep = lax.dynamic_index_in_dim(arrived, core, 1, keepdims=False)
    give = lax.dynamic_index_in_dim(arrived, 1 - core, 1, keepdims=False)
    got = lax.ppermute(give, "pair", swap)
    tiles = jnp.zeros((Y, PART, 4 * FREQS), F32)
    for t in range(2):
        tiles = lax.dynamic_update_index_in_dim(tiles, keep[t], (my_z - 2 * core - t) % Z, 0)
        tiles = lax.dynamic_update_index_in_dim(
            tiles, got[t], (my_z - 2 * (1 - core) - t) % Z, 0
        )
    return tiles.reshape(Y * PART, 4, FREQS).transpose(2, 1, 0)


def solution(mesh):
    placed = (P("pair", ("grow", "gcol")), P("pair", ("gcol", "grow")), P("pair"), P("pair"))
    return jax.shard_map(
        per_device,
        mesh=mesh,
        in_specs=placed,
        out_specs=P(None, "grow", ("gcol", "pair")),
        check_vma=False,
    )
```

time: 213 us -> 61.5 us (0.29); the launches traced: 210 us -> 61.2 us
  waiting for transfers between devices: 159 us -> 14.1 us
  local copies, waits for them, and re-layouts: 26.5 us -> 3.39 us
  starting transfers between devices: 0.04 us -> 17.7 us
  blocking collectives: 3.51 us -> 18.5 us
  between operations: 13.4 us -> 0.18 us
  matrix products: 7.41 us -> 0 us
  Pallas kernels: 0 us -> 5.19 us
    unnamed x3 -> x0, waiting for transfers between devices: 90.5 us -> none
    all_gather x1 -> x0, waiting for transfers between devices: 68.1 us -> none  [per_device(): lax.all_gather(column_density, 'grow', axis=1, tiled=True)]
    unnamed x3 -> x5, local copies, waits for them, and re-layouts: 25.4 us -> 1.43 us
    all_to_all x0 -> x1, blocking collectives: none -> 18.5 us  [per_device(): lax.all_to_all(jnp.concatenate([columns, meta], axis=1), 'pair', 0, 0, ax...]
    ppermute x0 -> x4, waiting for transfers between devices: none -> 9.71 us  [the longest x2 8.8 us: per_device(): lax.ppermute(summed[t], ('pair', 'grow'), [(((y * X + x) * CORES + c) * Z...]
    ppermute x0 -> x4, starting transfers between devices: none -> 9.48 us  [the longest x2 4.48 us: per_device(): lax.ppermute(summed[t], ('pair', 'grow'), [(((y * X + x) * CORES + c) * Z...]
    all_to_all x0 -> x1, starting transfers between devices: none -> 8.19 us  [per_device(): lax.all_to_all(jnp.broadcast_to(signed[None], (GR // 2, 2, pairs)), ('gro...]
    dot_general x2 -> x0, matrix products: 7.41 us -> none  [the longest x1 6.36 us: per_device(): lax.dot_general(weighted_left, lax.all_gather(column_density, 'grow', axi...]
  transfers between devices with their start and end apart: 2 -> 5, of which waited for: 2 -> 4; matrix products, arithmetic and copies ran while one was open for 1% -> 4% of each run, Pallas kernels for 0% -> 4%
where the time goes in v2:
time: 61.5 us; the launch traced here: 61.2 us
  blocking collectives  18.5 us (30%)
  starting transfers between devices  17.7 us (29%)
  waiting for transfers between devices  14.1 us (23%)
  Pallas kernels  5.19 us (8%)
  local copies, waits for them, and re-layouts  3.39 us (6%)
  other arithmetic  2.16 us (4%)
    all_to_all x1, blocking collectives, per_device(): lax.all_to_all(jnp.concatenate([columns, meta], axis=1), 'pair', 0, 0, ax...  18.5 us
    ppermute x2, waiting for transfers between devices, per_device(): lax.ppermute(summed[t], ('pair', 'grow'), [(((y * X + x) * CORES + c) * Z...  8.8 us
    all_to_all x1, starting transfers between devices, per_device(): lax.all_to_all(jnp.broadcast_to(signed[None], (GR // 2, 2, pairs)), ('gro...  8.19 us
    pallas_call x2, Pallas kernels, polarize_groups(): pl.pallas_call(functools.partial(polarize, groups), out_shape=jax.ShapeDt...  5.19 us
    ppermute x2, starting transfers between devices, per_device(): lax.ppermute(summed[t], ('pair', 'grow'), [(((y * X + x) * CORES + c) * Z...  4.48 us
    all_to_all x1, waiting for transfers between devices, per_device(): lax.all_to_all(jnp.broadcast_to(signed[None], (GR // 2, 2, pairs)), ('gro...  4.39 us
    ppermute x1, starting transfers between devices, per_device(): theirs = lax.ppermute(polarize_groups((2, 3), received), 'pair', swap)  3.4 us
    ppermute x1, starting transfers between devices, per_device(): got = lax.ppermute(give, 'pair', swap)  1.6 us
  transfers between devices with their start and end apart: 5, of which 4 were waited for; matrix products, arithmetic and copies ran while one was open for 4% of the time, Pallas kernels for 4%

profile of v2, /device:TPU:17, one launch (start us, length us, event | category | flops | bytes accessed | tf_op | source)
XLA Modules:
  0.0 61.2 jit_solution(14339684987447700067)
XLA Ops:
  0.0 0.7 %convert_element_type.7 = bf16[256]{0:T(256)(128)(2,1)S(1)} convert(s32[256]{0:T(256)} %param.9) | non-fusion elementwise | flops 256 | bytes 1536 | tf_op jit(solution)/shard_map/convert_element_type | solution.py:109
  0.7 0.7 %multiply_bitcast_fusion = bf16[2,256]{1,0:T(2,128)(2,1)S(1)} fusion(bf16[256,2]{0,1:T(2,128)(2,1)} %param.6, bf16[256]{0:T(256)(128)(2,1)S(1)} %convert_element_type.7), kind=kLoop, calls=%fused_computation.24 | loop fusion | flops 512 | bytes 2560 | tf_op jit(solution)/shard_map/transpose | solution.py:109
  1.4 0.6 broadcast_in_dim.13
  2.0 8.2 %all-to-all-start = ((bf16[8,2,256]{2,1,0:T(2,128)(2,1)}), bf16[8,2,256]{2,1,0:T(2,128)(2,1)S(1)}, u32[]{:S(2)}, u32[]{:S(2)}) async-start(bf16[8,2,256]{2,1,0:T(2,128)(2,1)} %broadcast_in_dim.13), calls=%async_computation | async-start | bytes 16384 | tf_op jit(solution)/shard_map/all_to_all | solution.py:110
  10.2 0.7 %convert_element_type.8 = bf16[256]{0:T(256)(128)(2,1)S(1)} convert(s32[256]{0:T(256)} %param.8) | non-fusion elementwise | flops 256 | bytes 1536 | tf_op jit(solution)/shard_map/convert_element_type | solution.py:118
  10.8 1.4 %copy.8 = bf16[256,1536]{0,1:T(8,128)(2,1)S(1)} copy(bf16[256,1536]{1,0:T(8,128)(2,1)} %param.7) | data formatting | bytes 1572864 | tf_op args[1]
  12.2 0.1 copy.9
  12.3 4.4 %all-to-all-done = bf16[8,2,256]{2,1,0:T(2,128)(2,1)S(1)} async-done(((bf16[8,2,256]{2,1,0:T(2,128)(2,1)}), bf16[8,2,256]{2,1,0:T(2,128)(2,1)S(1)}, u32[]{:S(2)}, u32[]{:S(2)}) %all-to-all-start) | async-done | bytes 8224 | tf_op jit(solution)/shard_map/all_to_all | solution.py:110
  16.9 0.1 pad_maximum_fusion
  17.0 0.0 copy-start
  17.0 18.5 %all_to_all.10.recv_ref = bf16[16,120,256]{2,1,0:T(8,128)(2,1)S(1)} all-to-all(bf16[16,120,256]{2,1,0:T(8,128)(2,1)S(1)} %pad_maximum_fusion), channel_id=1, replica_groups={{0,16,32,48,64,80,96,112,128,144,160,176,192,208,224,240},{8,24,40,56,7..., dimensions={0} | all-to-all | bytes 1966080 | tf_op jit(solution)/shard_map/all_to_all | solution.py:124
  35.6 0.0 copy-done
  35.6 2.6 %shard_map.65 = f32[2,96,256]{2,1,0:T(8,128)S(1)} custom-call(bf16[128,256]{1,0:T(8,128)(2,1)S(1)} %copy-done, bf16[16,120,256]{2,1,0:T(8,128)(2,1)S(1)} %all_to_all.10.recv_ref), custom_call_target="tpu_custom_call" | custom-call | flops 805306368 | bytes 983040 | tf_op jit(solution)/shard_map/pallas_call | solution.py:90
  38.2 3.4 %collective-permute-start = (f32[2,96,256]{2,1,0:T(8,128)S(1)}, f32[2,96,256]{2,1,0:T(8,128)S(1)}, u32[]{:S(2)}, u32[]{:S(2)}) collective-permute-start(f32[2,96,256]{2,1,0:T(8,128)S(1)} %shard_map.65), channel_id=1, source_target_pairs={{0,8},{8,0},{16,24},{24,16},{32,40},{40,32},{48,56},{56,48},{64,72... | collective-permute-start | bytes 589832 | tf_op jit(solution)/shard_map/ppermute | solution.py:136
  41.6 2.6 %shard_map.64 = f32[2,96,256]{2,1,0:T(8,128)S(1)} custom-call(bf16[128,256]{1,0:T(8,128)(2,1)S(1)} %copy-done, bf16[16,120,256]{2,1,0:T(8,128)(2,1)S(1)} %all_to_all.10.recv_ref), custom_call_target="tpu_custom_call" | custom-call | flops 805306368 | bytes 983040 | tf_op jit(solution)/shard_map/pallas_call | solution.py:90
  44.1 0.0 collective-permute-done
  44.2 4.3 %collective-permute-start.1 = (f32[96,256]{1,0:T(8,128)S(1)}, f32[96,256]{1,0:T(8,128)S(1)}, u32[]{:S(2)}, u32[]{:S(2)}) collective-permute-start(f32[96,256]{1,0:T(8,128)S(1)} %get-tuple-element.8), channel_id=1, source_target_pairs={{0,0},{2,64},{4,128},{6,192},{8,12},{10,76},{12,140},{14,204},{16,... | collective-permute-start | bytes 294920 | tf_op jit(solution)/shard_map/ppermute | solution.py:142
  48.5 0.2 collective-permute-start.2
  48.7 6.3 %collective-permute-done.1 = f32[96,256]{1,0:T(8,128)S(1)} collective-permute-done((f32[96,256]{1,0:T(8,128)S(1)}, f32[96,256]{1,0:T(8,128)S(1)}, u32[]{:S(2)}, u32[]{:S(2)}) %collective-permute-start.1) | collective-permute-done | bytes 98336 | tf_op jit(solution)/shard_map/ppermute | solution.py:142
  55.0 2.5 %collective-permute-done.2 = f32[96,256]{1,0:T(8,128)S(1)} collective-permute-done((f32[96,256]{1,0:T(8,128)S(1)}, f32[96,256]{1,0:T(8,128)S(1)}, u32[]{:S(2)}, u32[]{:S(2)}) %collective-permute-start.2) | collective-permute-done | bytes 98336 | tf_op jit(solution)/shard_map/ppermute | solution.py:142
  57.5 1.6 %collective-permute-start.3 = (f32[2,48,256]{2,1,0:T(8,128)S(1)}, f32[2,48,256]{2,1,0:T(8,128)S(1)}, u32[]{:S(2)}, u32[]{:S(2)}) collective-permute-start(f32[2,48,256]{2,1,0:T(8,128)S(1)} %get-tuple-element.5), channel_id=1, source_target_pairs={{0,8},{8,0},{16,24},{24,16},{32,40},{40,32},{48,56},{56,48},{64,72... | collective-permute-start | bytes 294920 | tf_op jit(solution)/shard_map/ppermute | solution.py:160
  59.2 0.9 %collective-permute-done.3 = f32[2,48,256]{2,1,0:T(8,128)S(1)} collective-permute-done((f32[2,48,256]{2,1,0:T(8,128)S(1)}, f32[2,48,256]{2,1,0:T(8,128)S(1)}, u32[]{:S(2)}, u32[]{:S(2)}) %collective-permute-start.3) | collective-permute-done | bytes 98336 | tf_op jit(solution)/shard_map/ppermute | solution.py:160
  60.1 0.2 reshape.40
  60.3 0.9 %copy.10 = f32[64,4,192]{2,1,0:T(4,128)} copy(f32[64,4,192]{0,1,2:T(4,128)S(1)} %bitcast.28) | data formatting | bytes 393216 | tf_op jit(solution)/shard_map/transpose | solution.py:167
  (20 shorter events, 0.2 us)
Async XLA Ops:
  2.0 14.8 %all-to-all-start = ((bf16[8,2,256]{2,1,0:T(2,128)(2,1)}), bf16[8,2,256]{2,1,0:T(2,128)(2,1)S(1)}, u32[]{:S(2)}, u32[]{:S(2)}) async-start(bf16[8,2,256]{2,1,0:T(2,128)(2,1)} %broadcast_in_dim.13), calls=%async_computation | async-start | bytes 16384 | tf_op jit(solution)/shard_map/all_to_all | solution.py:110
  17.0 18.5 %copy-start = (bf16[128,256]{1,0:T(8,128)(2,1)S(1)}, bf16[128,256]{1,0:T(8,128)(2,1)}, u32[]{:S(2)}) copy-start(bf16[128,256]{1,0:T(8,128)(2,1)} %constant.81.clone.table_ref) | copy-start | bytes 196612
  38.2 6.0 %collective-permute-start = (f32[2,96,256]{2,1,0:T(8,128)S(1)}, f32[2,96,256]{2,1,0:T(8,128)S(1)}, u32[]{:S(2)}, u32[]{:S(2)}) collective-permute-start(f32[2,96,256]{2,1,0:T(8,128)S(1)} %shard_map.65), channel_id=1, source_target_pairs={{0,8},{8,0},{16,24},{24,16},{32,40},{40,32},{48,56},{56,48},{64,72... | collective-permute-start | bytes 589832 | tf_op jit(solution)/shard_map/ppermute | solution.py:136
  44.2 10.8 %collective-permute-start.1 = (f32[96,256]{1,0:T(8,128)S(1)}, f32[96,256]{1,0:T(8,128)S(1)}, u32[]{:S(2)}, u32[]{:S(2)}) collective-permute-start(f32[96,256]{1,0:T(8,128)S(1)} %get-tuple-element.8), channel_id=1, source_target_pairs={{0,0},{2,64},{4,128},{6,192},{8,12},{10,76},{12,140},{14,204},{16,... | collective-permute-start | bytes 294920 | tf_op jit(solution)/shard_map/ppermute | solution.py:142
  48.5 9.0 %collective-permute-start.2 = (f32[96,256]{1,0:T(8,128)S(1)}, f32[96,256]{1,0:T(8,128)S(1)}, u32[]{:S(2)}, u32[]{:S(2)}) collective-permute-start(f32[96,256]{1,0:T(8,128)S(1)} %get-tuple-element.7), channel_id=1, source_target_pairs={{0,2},{2,66},{4,130},{6,194},{8,14},{10,78},{12,142},{14,206},{16,... | collective-permute-start | bytes 294920 | tf_op jit(solution)/shard_map/ppermute | solution.py:142
  57.5 2.5 %collective-permute-start.3 = (f32[2,48,256]{2,1,0:T(8,128)S(1)}, f32[2,48,256]{2,1,0:T(8,128)S(1)}, u32[]{:S(2)}, u32[]{:S(2)}) collective-permute-start(f32[2,48,256]{2,1,0:T(8,128)S(1)} %get-tuple-element.5), channel_id=1, source_target_pairs={{0,8},{8,0},{16,24},{24,16},{32,40},{40,32},{48,56},{56,48},{64,72... | collective-permute-start | bytes 294920 | tf_op jit(solution)/shard_map/ppermute | solution.py:160

commit v3 on v2

--- a/solution.py
+++ b/solution.py
@@ -16,8 +16,7 @@
 CORES = 2
 Z = 4
 CHIPS = Y * X
-PART = 48
-COLS = CORES * PART
+COLS = 96
 META = GR + 8
 STEP = 4
 BF16 = jnp.bfloat16
@@ -106,21 +105,25 @@
     core = me % CORES
     my_z = lax.axis_index("grow")
 
-    signed = (slab_density * occupation[:, None].astype(BF16)).T
     slabs = lax.all_to_all(
-        jnp.broadcast_to(signed[None], (GR // 2, 2, pairs)), ("grow", "gcol"), 0, 0, tiled=True
-    ).reshape(Z, 4, pairs)
+        jnp.broadcast_to(slab_density.T[None], (GR // 2, 2, pairs)),
+        ("grow", "gcol"),
+        0,
+        0,
+        tiled=True,
+    )
+    slabs = slabs.reshape(Z, 4, pairs) * occupation[None, None, :].astype(BF16)
 
-    twice = jnp.concatenate([slabs, slabs, slabs], axis=0)
+    thrice = jnp.concatenate([slabs, slabs, slabs], axis=0)
     turned = jnp.stack(
-        [lax.dynamic_slice_in_dim(twice, y + 2 * core, Z, 0) for y in range(Y)]
+        [lax.dynamic_slice_in_dim(thrice, 4 + 2 * core - y, Z, 0) for y in range(Y)]
     ).reshape(Y, GR, pairs)
     bins = jnp.broadcast_to(bin_index.astype(BF16)[None, None, :], (Y, META - GR, pairs))
     meta = jnp.concatenate([turned, bins], axis=1)
     meta = jnp.broadcast_to(meta[:, None], (Y, X, META, pairs)).reshape(CHIPS, META, pairs)
 
-    columns = column_density.T.reshape(X, CORES, Y, PART, pairs)
-    columns = columns.transpose(2, 0, 1, 3, 4).reshape(CHIPS, COLS, pairs)
+    columns = column_density.T.reshape(X, Y, COLS, pairs)
+    columns = columns.transpose(1, 0, 2, 3).reshape(CHIPS, COLS, pairs)
     received = lax.all_to_all(
         jnp.concatenate([columns, meta], axis=1),
         "pair",
@@ -145,7 +148,7 @@
                 [
                     (
                         ((y * X + x) * CORES + c) * Z + z,
-                        ((z * X + x) * CORES + c) * Z + (y + 2 * c + t) % Z,
+                        ((z * X + x) * CORES + y // 2) * Z + (2 * c + t - y) % Z,
                     )
                     for y in range(Y)
                     for x in range(X)
@@ -154,17 +157,12 @@
                 ],
             )
         )
-    arrived = jnp.stack(arrived).reshape(2, CORES, PART, 4 * FREQS)
-    keep = lax.dynamic_index_in_dim(arrived, core, 1, keepdims=False)
-    give = lax.dynamic_index_in_dim(arrived, 1 - core, 1, keepdims=False)
-    got = lax.ppermute(give, "pair", swap)
-    tiles = jnp.zeros((Y, PART, 4 * FREQS), F32)
-    for t in range(2):
-        tiles = lax.dynamic_update_index_in_dim(tiles, keep[t], (my_z - 2 * core - t) % Z, 0)
-        tiles = lax.dynamic_update_index_in_dim(
-            tiles, got[t], (my_z - 2 * (1 - core) - t) % Z, 0
-        )
-    return tiles.reshape(Y * PART, 4, FREQS).transpose(2, 1, 0)
+    tiles = jnp.where(
+        my_z % 2 == 0,
+        jnp.concatenate(arrived, axis=0),
+        jnp.concatenate(arrived[::-1], axis=0),
+    )
+    return tiles.reshape(CORES * COLS, 4, FREQS).transpose(2, 1, 0)
 
 
 def solution(mesh):

time: 61.5 us -> 59.9 us (0.974)
  the two profiles are of different devices: /device:TPU:17 before, /device:TPU:16 now
where the time goes in v3:
time: 59.9 us; the launch traced here: 59.6 us
  blocking collectives  19.7 us (33%)
  starting transfers between devices  15.1 us (25%)
  waiting for transfers between devices  13.7 us (23%)
  Pallas kernels  5.19 us (9%)
  local copies, waits for them, and re-layouts  3.91 us (7%)
  other arithmetic  1.7 us (3%)
    all_to_all x1, blocking collectives, per_device(): lax.all_to_all(jnp.concatenate([columns, meta], axis=1), 'pair', 0, 0, ax...  19.7 us
    ppermute x2, waiting for transfers between devices, per_device(): lax.ppermute(summed[t], ('pair', 'grow'), [(((y * X + x) * CORES + c) * Z...  8.85 us
    all_to_all x1, starting transfers between devices, per_device(): lax.all_to_all(jnp.broadcast_to(slab_density.T[None], (GR // 2, 2, pairs)...  8.47 us
    ppermute x2, starting transfers between devices, per_device(): lax.ppermute(summed[t], ('pair', 'grow'), [(((y * X + x) * CORES + c) * Z...  6.57 us
    pallas_call x2, Pallas kernels, polarize_groups(): pl.pallas_call(functools.partial(polarize, groups), out_shape=jax.ShapeDt...  5.19 us
    all_to_all x1, waiting for transfers between devices, per_device(): lax.all_to_all(jnp.broadcast_to(slab_density.T[None], (GR // 2, 2, pairs)...  4.89 us
    unnamed x3, local copies, waits for them, and re-layouts  1.41 us
    broadcast_in_dim x1, local copies, waits for them, and re-layouts, per_device(): jnp.broadcast_to(slab_density.T[None], (GR // 2, 2, pairs))  1.28 us
  transfers between devices with their start and end apart: 4, of which 3 were waited for; matrix products, arithmetic and copies ran while one was open for 5% of the time, Pallas kernels for 4%

profile of v3, /device:TPU:16, one launch (start us, length us, event | category | flops | bytes accessed | tf_op | source)
XLA Modules:
  0.0 59.6 jit_solution(11278977178322765720)
XLA Ops:
  0.0 1.3 %broadcast_in_dim.6 = bf16[8,2,256]{2,1,0:T(2,128)(2,1)} broadcast(bf16[2,256]{1,0:T(2,128)(2,1)} %bitcast.21), dimensions={1,2} | broadcast | bytes 9216 | tf_op jit(solution)/shard_map/broadcast_in_dim | solution.py:109
  1.3 8.5 %all-to-all-start = ((bf16[8,2,256]{2,1,0:T(2,128)(2,1)}), bf16[8,2,256]{2,1,0:T(2,128)(2,1)S(1)}, u32[]{:S(2)}, u32[]{:S(2)}) async-start(bf16[8,2,256]{2,1,0:T(2,128)(2,1)} %broadcast_in_dim.6), calls=%async_computation | async-start | bytes 16384 | tf_op jit(solution)/shard_map/all_to_all | solution.py:108
  9.7 0.7 %convert_element_type.8 = bf16[256]{0:T(256)(128)(2,1)S(1)} convert(s32[256]{0:T(256)} %param.8) | non-fusion elementwise | flops 256 | bytes 1536 | tf_op jit(solution)/shard_map/convert_element_type | solution.py:121
  10.4 0.7 %convert_element_type.7 = bf16[256]{0:T(256)(128)(2,1)S(1)} convert(s32[256]{0:T(256)} %param.9) | non-fusion elementwise | flops 256 | bytes 1536 | tf_op jit(solution)/shard_map/convert_element_type | solution.py:115
  11.1 1.4 %copy.12 = bf16[256,1536]{0,1:T(8,128)(2,1)S(1)} copy(bf16[256,1536]{1,0:T(8,128)(2,1)} %param.7) | data formatting | bytes 1572864 | tf_op args[1]
  12.5 0.1 copy.13
  12.6 4.9 %all-to-all-done = bf16[8,2,256]{2,1,0:T(2,128)(2,1)S(1)} async-done(((bf16[8,2,256]{2,1,0:T(2,128)(2,1)}), bf16[8,2,256]{2,1,0:T(2,128)(2,1)S(1)}, u32[]{:S(2)}, u32[]{:S(2)}) %all-to-all-start) | async-done | bytes 8224 | tf_op jit(solution)/shard_map/all_to_all | solution.py:108
  17.7 0.1 pad_maximum_fusion
  17.7 0.0 copy-start
  17.8 19.7 %all_to_all.10.recv_ref = bf16[16,120,256]{2,1,0:T(8,128)(2,1)S(1)} all-to-all(bf16[16,120,256]{2,1,0:T(8,128)(2,1)S(1)} %pad_maximum_fusion), channel_id=1, replica_groups={{0,16,32,48,64,80,96,112,128,144,160,176,192,208,224,240},{8,24,40,56,7..., dimensions={0} | all-to-all | bytes 1966080 | tf_op jit(solution)/shard_map/all_to_all | solution.py:127
  37.5 0.0 copy-done
  37.5 2.6 %shard_map.65 = f32[2,96,256]{2,1,0:T(8,128)S(1)} custom-call(bf16[128,256]{1,0:T(8,128)(2,1)S(1)} %copy-done, bf16[16,120,256]{2,1,0:T(8,128)(2,1)S(1)} %all_to_all.10.recv_ref), custom_call_target="tpu_custom_call" | custom-call | flops 805306368 | bytes 983040 | tf_op jit(solution)/shard_map/pallas_call | solution.py:89
  40.1 0.1 collective-permute-start
  40.2 2.6 %shard_map.64 = f32[2,96,256]{2,1,0:T(8,128)S(1)} custom-call(bf16[128,256]{1,0:T(8,128)(2,1)S(1)} %copy-done, bf16[16,120,256]{2,1,0:T(8,128)(2,1)S(1)} %all_to_all.10.recv_ref), custom_call_target="tpu_custom_call" | custom-call | flops 805306368 | bytes 983040 | tf_op jit(solution)/shard_map/pallas_call | solution.py:89
  42.8 0.0 collective-permute-done
  42.9 6.0 %collective-permute-start.1 = (f32[96,256]{1,0:T(8,128)S(1)}, f32[96,256]{1,0:T(8,128)S(1)}, u32[]{:S(2)}, u32[]{:S(2)}) collective-permute-start(f32[96,256]{1,0:T(8,128)S(1)} %get-tuple-element.5), channel_id=1, source_target_pairs={{0,0},{2,64},{4,128},{6,192},{8,4},{10,68},{12,132},{14,196},{16,1... | collective-permute-start | bytes 294920 | tf_op jit(solution)/shard_map/ppermute | solution.py:145
  48.9 0.6 collective-permute-start.2
  49.4 6.9 %collective-permute-done.1 = f32[96,256]{1,0:T(8,128)S(1)} collective-permute-done((f32[96,256]{1,0:T(8,128)S(1)}, f32[96,256]{1,0:T(8,128)S(1)}, u32[]{:S(2)}, u32[]{:S(2)}) %collective-permute-start.1) | collective-permute-done | bytes 98336 | tf_op jit(solution)/shard_map/ppermute | solution.py:145
  56.3 0.1 copy.14
  56.4 2.0 %collective-permute-done.2 = f32[96,256]{1,0:T(8,128)S(1)} collective-permute-done((f32[96,256]{1,0:T(8,128)S(1)}, f32[96,256]{1,0:T(8,128)S(1)}, u32[]{:S(2)}, u32[]{:S(2)}) %collective-permute-start.2) | collective-permute-done | bytes 98336 | tf_op jit(solution)/shard_map/ppermute | solution.py:145
  58.4 0.1 copy.15
  58.5 0.2 fusion
  58.7 0.9 %copy.16 = f32[64,4,192]{2,1,0:T(4,128)} copy(f32[64,4,192]{2,0,1:T(8,128)S(1)} %fusion) | data formatting | bytes 393216 | tf_op jit(solution)/shard_map/transpose | solution.py:165
  (13 shorter events, 0.2 us)
Async XLA Ops:
  1.3 16.2 %all-to-all-start = ((bf16[8,2,256]{2,1,0:T(2,128)(2,1)}), bf16[8,2,256]{2,1,0:T(2,128)(2,1)S(1)}, u32[]{:S(2)}, u32[]{:S(2)}) async-start(bf16[8,2,256]{2,1,0:T(2,128)(2,1)} %broadcast_in_dim.6), calls=%async_computation | async-start | bytes 16384 | tf_op jit(solution)/shard_map/all_to_all | solution.py:108
  17.7 19.7 %copy-start = (bf16[128,256]{1,0:T(8,128)(2,1)S(1)}, bf16[128,256]{1,0:T(8,128)(2,1)}, u32[]{:S(2)}) copy-start(bf16[128,256]{1,0:T(8,128)(2,1)} %constant.51.clone.table_ref) | copy-start | bytes 196612
  40.1 2.7 %collective-permute-start = (f32[2,96,256]{2,1,0:T(8,128)S(1)}, f32[2,96,256]{2,1,0:T(8,128)S(1)}, u32[]{:S(2)}, u32[]{:S(2)}) collective-permute-start(f32[2,96,256]{2,1,0:T(8,128)S(1)} %shard_map.65), channel_id=1, source_target_pairs={{0,8},{8,0},{16,24},{24,16},{32,40},{40,32},{48,56},{56,48},{64,72... | collective-permute-start | bytes 589832 | tf_op jit(solution)/shard_map/ppermute | solution.py:139
  42.9 13.5 %collective-permute-start.1 = (f32[96,256]{1,0:T(8,128)S(1)}, f32[96,256]{1,0:T(8,128)S(1)}, u32[]{:S(2)}, u32[]{:S(2)}) collective-permute-start(f32[96,256]{1,0:T(8,128)S(1)} %get-tuple-element.5), channel_id=1, source_target_pairs={{0,0},{2,64},{4,128},{6,192},{8,4},{10,68},{12,132},{14,196},{16,1... | collective-permute-start | bytes 294920 | tf_op jit(solution)/shard_map/ppermute | solution.py:145
  48.9 9.5 %collective-permute-start.2 = (f32[96,256]{1,0:T(8,128)S(1)}, f32[96,256]{1,0:T(8,128)S(1)}, u32[]{:S(2)}, u32[]{:S(2)}) collective-permute-start(f32[96,256]{1,0:T(8,128)S(1)} %get-tuple-element.6), channel_id=1, source_target_pairs={{0,2},{2,66},{4,130},{6,194},{8,6},{10,70},{12,134},{14,198},{16,1... | collective-permute-start | bytes 294920 | tf_op jit(solution)/shard_map/ppermute | solution.py:145

commit v4 on v3

--- a/solution.py
+++ b/solution.py
@@ -19,6 +19,13 @@
 COLS = 96
 META = GR + 8
 STEP = 4
+DISTANCE = (
+    ((1, 3), (0, 2)),
+    ((0, 2), (1, 3)),
+    ((2, 1), (3, 0)),
+    ((2, 1), (3, 0)),
+)
+HALVES = ((0, 3), (1, 2))
 BF16 = jnp.bfloat16
 F32 = jnp.float32
 
@@ -103,6 +110,7 @@
     pairs = slab_density.shape[0]
     me = lax.axis_index("pair")
     core = me % CORES
+    my_y = me // (X * CORES)
     my_z = lax.axis_index("grow")
 
     slabs = lax.all_to_all(
@@ -114,18 +122,24 @@
     )
     slabs = slabs.reshape(Z, 4, pairs) * occupation[None, None, :].astype(BF16)
 
-    thrice = jnp.concatenate([slabs, slabs, slabs], axis=0)
-    turned = jnp.stack(
-        [lax.dynamic_slice_in_dim(thrice, 4 + 2 * core - y, Z, 0) for y in range(Y)]
-    ).reshape(Y, GR, pairs)
-    bins = jnp.broadcast_to(bin_index.astype(BF16)[None, None, :], (Y, META - GR, pairs))
-    meta = jnp.concatenate([turned, bins], axis=1)
-    meta = jnp.broadcast_to(meta[:, None], (Y, X, META, pairs)).reshape(CHIPS, META, pairs)
-
+    slabs = lax.dynamic_slice_in_dim(jnp.concatenate([slabs, slabs], axis=0), my_z, Z, 0)
+    bins = jnp.broadcast_to(bin_index.astype(BF16)[None, :], (META - GR, pairs))
     columns = column_density.T.reshape(X, Y, COLS, pairs)
-    columns = columns.transpose(1, 0, 2, 3).reshape(CHIPS, COLS, pairs)
+    payload = []
+    for step in range(Y):
+        keep, give = DISTANCE[step]
+        meta = jnp.where(
+            core == 0,
+            jnp.concatenate([slabs[i] for i in keep + give] + [bins], axis=0),
+            jnp.concatenate([slabs[i] for i in give + keep] + [bins], axis=0),
+        )
+        part = next(2 * c + HALVES[c].index(step) for c in range(CORES) if step in HALVES[c])
+        payload.append(
+            jnp.concatenate([columns[:, part], jnp.broadcast_to(meta[None], (X, META, pairs))], axis=1)
+        )
+    payload = lax.dynamic_slice_in_dim(jnp.stack(payload + payload), (Y - my_z) % Y, Y, 0)
     received = lax.all_to_all(
-        jnp.concatenate([columns, meta], axis=1),
+        payload.reshape(CHIPS, COLS + META, pairs),
         "pair",
         0,
         0,
@@ -141,24 +155,25 @@
 
     arrived = []
     for t in range(2):
-        arrived.append(
-            lax.ppermute(
-                summed[t],
-                ("pair", "grow"),
-                [
-                    (
-                        ((y * X + x) * CORES + c) * Z + z,
-                        ((z * X + x) * CORES + y // 2) * Z + (2 * c + t - y) % Z,
-                    )
-                    for y in range(Y)
-                    for x in range(X)
-                    for c in range(CORES)
-                    for z in range(Z)
-                ],
-            )
-        )
+        moves = []
+        for y in range(Y):
+            for z in range(Z):
+                step = (y - z) % Y
+                to_core = 0 if step in HALVES[0] else 1
+                for x in range(X):
+                    for c in range(CORES):
+                        source = ((y * X + x) * CORES + c) * Z + z
+                        target = ((z * X + x) * CORES + to_core) * Z
+                        moves.append((source, target + (z + DISTANCE[step][c][t]) % Z))
+        arrived.append(lax.ppermute(summed[t], ("pair", "grow"), moves))
+    first = np.zeros((CORES, Z), np.int32)
+    for c in range(CORES):
+        for half in range(2):
+            for group in DISTANCE[HALVES[c][half]]:
+                first[c, group[0]] = half
+    my_first = jnp.asarray(first.reshape(-1))[core * Z + (my_z - my_y) % Z]
     tiles = jnp.where(
-        my_z % 2 == 0,
+        my_first == 0,
         jnp.concatenate(arrived, axis=0),
         jnp.concatenate(arrived[::-1], axis=0),
     )

time: 59.9 us -> 57.6 us (0.962)
  the two profiles are of different devices: /device:TPU:16 before, /device:TPU:17 now
where the time goes in v4:
time: 57.6 us; the launch traced here: 56.8 us
  blocking collectives  18.4 us (32%)
  starting transfers between devices  14.5 us (25%)
  waiting for transfers between devices  12.6 us (22%)
  Pallas kernels  5.19 us (9%)
  local copies, waits for them, and re-layouts  4.73 us (8%)
  between operations  0.91 us (2%)
    all_to_all x1, blocking collectives, per_device(): lax.all_to_all(payload.reshape(CHIPS, COLS + META, pairs), 'pair', 0, 0,...  18.4 us
    all_to_all x1, starting transfers between devices, per_device(): lax.all_to_all(jnp.broadcast_to(slab_density.T[None], (GR // 2, 2, pairs)...  8.19 us
    ppermute x2, waiting for transfers between devices, per_device(): arrived.append(lax.ppermute(summed[t], ('pair', 'grow'), moves))  7.6 us
    pallas_call x2, Pallas kernels, polarize_groups(): pl.pallas_call(functools.partial(polarize, groups), out_shape=jax.ShapeDt...  5.19 us
    all_to_all x1, waiting for transfers between devices, per_device(): lax.all_to_all(jnp.broadcast_to(slab_density.T[None], (GR // 2, 2, pairs)...  5.03 us
    ppermute x1, starting transfers between devices, per_device(): theirs = lax.ppermute(polarize_groups((2, 3), received), 'pair', swap)  3.39 us
    ppermute x2, starting transfers between devices, per_device(): arrived.append(lax.ppermute(summed[t], ('pair', 'grow'), moves))  2.94 us
    unnamed x9, local copies, waits for them, and re-layouts  1.42 us
  transfers between devices with their start and end apart: 4, of which 3 were waited for; matrix products, arithmetic and copies ran while one was open for 4% of the time, Pallas kernels for 5%

profile of v4, /device:TPU:17, one launch (start us, length us, event | category | flops | bytes accessed | tf_op | source)
XLA Modules:
  0.0 56.8 jit_solution(10455506916641126891)
XLA Ops:
  0.0 0.0 copy-start.1
  0.0 0.0 copy-start.2
  0.0 1.3 %broadcast_in_dim.10 = bf16[8,2,256]{2,1,0:T(2,128)(2,1)} broadcast(bf16[2,256]{1,0:T(2,128)(2,1)} %bitcast.64), dimensions={1,2} | broadcast | bytes 9216 | tf_op jit(solution)/shard_map/broadcast_in_dim | solution.py:117
  1.3 8.2 %all-to-all-start = ((bf16[8,2,256]{2,1,0:T(2,128)(2,1)}), bf16[8,2,256]{2,1,0:T(2,128)(2,1)S(1)}, u32[]{:S(2)}, u32[]{:S(2)}) async-start(bf16[8,2,256]{2,1,0:T(2,128)(2,1)} %broadcast_in_dim.10), calls=%async_computation | async-start | bytes 16384 | tf_op jit(solution)/shard_map/all_to_all | solution.py:116
  9.5 1.4 %copy.16 = bf16[256,1536]{0,1:T(8,128)(2,1)S(1)} copy(bf16[256,1536]{1,0:T(8,128)(2,1)} %param.8) | data formatting | bytes 1572864 | tf_op args[1]
  10.9 0.1 slice_bitcast_fusion
  11.0 0.0 copy-done.1
  11.0 0.0 copy-done.2
  11.0 5.0 %all-to-all-done = bf16[8,2,256]{2,1,0:T(2,128)(2,1)S(1)} async-done(((bf16[8,2,256]{2,1,0:T(2,128)(2,1)}), bf16[8,2,256]{2,1,0:T(2,128)(2,1)S(1)}, u32[]{:S(2)}, u32[]{:S(2)}) %all-to-all-start) | async-done | bytes 8224 | tf_op jit(solution)/shard_map/all_to_all | solution.py:116
  16.6 0.0 copy-start
  16.6 0.1 constant_dynamic-slice_fusion
  16.7 18.4 %all_to_all.10.recv_ref = bf16[16,120,256]{2,1,0:T(8,128)(2,1)S(1)} all-to-all(bf16[16,120,256]{2,1,0:T(8,128)(2,1)S(1)} %bitcast.60), channel_id=1, replica_groups={{0,16,32,48,64,80,96,112,128,144,160,176,192,208,224,240},{8,24,40,56,7..., dimensions={0} | all-to-all | bytes 1966080 | tf_op jit(solution)/shard_map/all_to_all | solution.py:141
  35.1 0.0 copy-done
  35.1 2.6 %shard_map.74 = f32[2,96,256]{2,1,0:T(8,128)S(1)} custom-call(bf16[128,256]{1,0:T(8,128)(2,1)S(1)} %copy-done, bf16[16,120,256]{2,1,0:T(8,128)(2,1)S(1)} %all_to_all.10.recv_ref), custom_call_target="tpu_custom_call" | custom-call | flops 805306368 | bytes 983040 | tf_op jit(solution)/shard_map/pallas_call | solution.py:96
  37.7 0.0 copy-start.3
  37.7 3.4 %collective-permute-start = (f32[2,96,256]{2,1,0:T(8,128)S(1)}, f32[2,96,256]{2,1,0:T(8,128)S(1)}, u32[]{:S(2)}, u32[]{:S(2)}) collective-permute-start(f32[2,96,256]{2,1,0:T(8,128)S(1)} %shard_map.74), channel_id=1, source_target_pairs={{0,8},{8,0},{16,24},{24,16},{32,40},{40,32},{48,56},{56,48},{64,72... | collective-permute-start | bytes 589832 | tf_op jit(solution)/shard_map/ppermute | solution.py:153
  41.1 2.6 %shard_map.73 = f32[2,96,256]{2,1,0:T(8,128)S(1)} custom-call(bf16[128,256]{1,0:T(8,128)(2,1)S(1)} %copy-done, bf16[16,120,256]{2,1,0:T(8,128)(2,1)S(1)} %all_to_all.10.recv_ref), custom_call_target="tpu_custom_call" | custom-call | flops 805306368 | bytes 983040 | tf_op jit(solution)/shard_map/pallas_call | solution.py:96
  43.7 0.0 collective-permute-done
  43.8 2.9 %collective-permute-start.1 = (f32[96,256]{1,0:T(8,128)S(1)}, f32[96,256]{1,0:T(8,128)S(1)}, u32[]{:S(2)}, u32[]{:S(2)}) collective-permute-start(f32[96,256]{1,0:T(8,128)S(1)} %get-tuple-element.9), channel_id=1, source_target_pairs={{0,2},{8,0},{16,18},{24,16},{32,34},{40,32},{48,50},{56,48},{2,70}... | collective-permute-start | bytes 294920 | tf_op jit(solution)/shard_map/ppermute | solution.py:168
  46.7 0.0 collective-permute-start.2
  46.7 0.0 copy-done.3
  46.7 0.6 %dynamic_slice.9 = s32[1]{0:T(128)} dynamic-slice(s32[8]{0:T(128)S(1)} %copy-done.3, s32[]{:T(128)S(6)} %select_n.70), dynamic_slice_sizes={1} | dynamic-slice | bytes 12 | tf_op jit(solution)/shard_map/dynamic_slice | solution.py:174
  48.0 7.2 %collective-permute-done.1 = f32[96,256]{1,0:T(8,128)S(1)} collective-permute-done((f32[96,256]{1,0:T(8,128)S(1)}, f32[96,256]{1,0:T(8,128)S(1)}, u32[]{:S(2)}, u32[]{:S(2)}) %collective-permute-start.1) | collective-permute-done | bytes 98336 | tf_op jit(solution)/shard_map/ppermute | solution.py:168
  55.2 0.1 copy.20
  55.3 0.4 collective-permute-done.2
  55.7 0.1 copy.21
  55.8 0.2 fusion
  56.0 0.9 %copy.22 = f32[64,4,192]{2,1,0:T(4,128)} copy(f32[64,4,192]{2,0,1:T(8,128)S(1)} %fusion) | data formatting | bytes 393216 | tf_op jit(solution)/shard_map/transpose | solution.py:180
  (25 shorter events, 0.5 us)
Async XLA Ops:
  0.0 11.0 %copy-start.1 = (s32[256]{0:T(256)S(1)}, s32[256]{0:T(256)}, u32[]{:S(2)}) copy-start(s32[256]{0:T(256)} %param.9) | copy-start | bytes 3076
  0.0 11.0 %copy-start.2 = (s32[256]{0:T(256)S(1)}, s32[256]{0:T(256)}, u32[]{:S(2)}) copy-start(s32[256]{0:T(256)} %param.10) | copy-start | bytes 3076
  1.3 14.8 %all-to-all-start = ((bf16[8,2,256]{2,1,0:T(2,128)(2,1)}), bf16[8,2,256]{2,1,0:T(2,128)(2,1)S(1)}, u32[]{:S(2)}, u32[]{:S(2)}) async-start(bf16[8,2,256]{2,1,0:T(2,128)(2,1)} %broadcast_in_dim.10), calls=%async_computation | async-start | bytes 16384 | tf_op jit(solution)/shard_map/all_to_all | solution.py:116
  16.6 18.5 %copy-start = (bf16[128,256]{1,0:T(8,128)(2,1)S(1)}, bf16[128,256]{1,0:T(8,128)(2,1)}, u32[]{:S(2)}) copy-start(bf16[128,256]{1,0:T(8,128)(2,1)} %constant.59.clone.table_ref) | copy-start | bytes 196612
  37.7 9.0 %copy-start.3 = (s32[8]{0:T(128)S(1)}, s32[8]{0:T(128)}, u32[]{:S(2)}) copy-start(s32[8]{0:T(128)} %constant.60.clone) | copy-start | bytes 100
  37.7 6.0 %collective-permute-start = (f32[2,96,256]{2,1,0:T(8,128)S(1)}, f32[2,96,256]{2,1,0:T(8,128)S(1)}, u32[]{:S(2)}, u32[]{:S(2)}) collective-permute-start(f32[2,96,256]{2,1,0:T(8,128)S(1)} %shard_map.74), channel_id=1, source_target_pairs={{0,8},{8,0},{16,24},{24,16},{32,40},{40,32},{48,56},{56,48},{64,72... | collective-permute-start | bytes 589832 | tf_op jit(solution)/shard_map/ppermute | solution.py:153
  43.8 11.4 %collective-permute-start.1 = (f32[96,256]{1,0:T(8,128)S(1)}, f32[96,256]{1,0:T(8,128)S(1)}, u32[]{:S(2)}, u32[]{:S(2)}) collective-permute-start(f32[96,256]{1,0:T(8,128)S(1)} %get-tuple-element.9), channel_id=1, source_target_pairs={{0,2},{8,0},{16,18},{24,16},{32,34},{40,32},{48,50},{56,48},{2,70}... | collective-permute-start | bytes 294920 | tf_op jit(solution)/shard_map/ppermute | solution.py:168
  46.7 8.9 %collective-permute-start.2 = (f32[96,256]{1,0:T(8,128)S(1)}, f32[96,256]{1,0:T(8,128)S(1)}, u32[]{:S(2)}, u32[]{:S(2)}) collective-permute-start(f32[96,256]{1,0:T(8,128)S(1)} %get-tuple-element.10), channel_id=1, source_target_pairs={{0,6},{8,4},{16,22},{24,20},{32,38},{40,36},{48,54},{56,52},{2,68}... | collective-permute-start | bytes 294920 | tf_op jit(solution)/shard_map/ppermute | solution.py:168

commit v5 on v4

--- a/solution.py
+++ b/solution.py
@@ -26,6 +26,7 @@
     ((2, 1), (3, 0)),
 )
 HALVES = ((0, 3), (1, 2))
+ORDER = ((2, 3), (1, 2), (1, 3), (1, 1), (2, 0), (3, 3), (0, 2), (3, 2), (0, 3), (2, 1), (3, 1), (1, 0), (3, 0), (0, 1), (2, 2), (0, 0))
 BF16 = jnp.bfloat16
 F32 = jnp.float32
 
@@ -139,12 +140,12 @@
         )
     payload = lax.dynamic_slice_in_dim(jnp.stack(payload + payload), (Y - my_z) % Y, Y, 0)
     received = lax.all_to_all(
-        payload.reshape(CHIPS, COLS + META, pairs),
+        jnp.stack([payload[y, x] for y, x in ORDER]),
         "pair",
         0,
         0,
         axis_index_groups=[
-            [(y * X + x) * CORES + c for y in range(Y) for x in range(X)] for c in range(CORES)
+            [(y * X + x) * CORES + c for y, x in ORDER] for c in range(CORES)
         ],
         tiled=True,
     )

time: 57.6 us -> 56.2 us (0.976)
  starting transfers between devices: 14.5 us -> 12.1 us
  waiting for transfers between devices: 12.6 us -> 14.3 us
  blocking collectives: 18.4 us -> 17.6 us
    ppermute x2, starting transfers between devices: 2.94 us -> 0.97 us  [per_device(): arrived.append(lax.ppermute(summed[t], ('pair', 'grow'), moves))]
    ppermute x2, waiting for transfers between devices: 7.6 us -> 9.25 us  [per_device(): arrived.append(lax.ppermute(summed[t], ('pair', 'grow'), moves))]
    all_to_all x1, blocking collectives: 18.4 us -> 17.6 us  [per_device(): lax.all_to_all(jnp.stack([payload[y, x] for y, x in ORDER]), 'pair', 0, 0...]
    unnamed x9 -> x24, local copies, waits for them, and re-layouts: 1.42 us -> 1.65 us
where the time goes in v5:
time: 56.2 us; the launch traced here: 55.6 us
  blocking collectives  17.6 us (31%)
  waiting for transfers between devices  14.3 us (25%)
  starting transfers between devices  12.1 us (22%)
  Pallas kernels  5.19 us (9%)
  local copies, waits for them, and re-layouts  4.9 us (9%)
  between operations  1.03 us (2%)
    all_to_all x1, blocking collectives, per_device(): lax.all_to_all(jnp.stack([payload[y, x] for y, x in ORDER]), 'pair', 0, 0...  17.6 us
    ppermute x2, waiting for transfers between devices, per_device(): arrived.append(lax.ppermute(summed[t], ('pair', 'grow'), moves))  9.25 us
    all_to_all x1, starting transfers between devices, per_device(): lax.all_to_all(jnp.broadcast_to(slab_density.T[None], (GR // 2, 2, pairs)...  8.19 us
    pallas_call x2, Pallas kernels, polarize_groups(): pl.pallas_call(functools.partial(polarize, groups), out_shape=jax.ShapeDt...  5.19 us
    all_to_all x1, waiting for transfers between devices, per_device(): lax.all_to_all(jnp.broadcast_to(slab_density.T[None], (GR // 2, 2, pairs)...  5.03 us
    ppermute x1, starting transfers between devices, per_device(): theirs = lax.ppermute(polarize_groups((2, 3), received), 'pair', swap)  2.97 us
    unnamed x24, local copies, waits for them, and re-layouts  1.65 us
    broadcast_in_dim x1, local copies, waits for them, and re-layouts, per_device(): jnp.broadcast_to(slab_density.T[None], (GR // 2, 2, pairs))  1.31 us
  transfers between devices with their start and end apart: 4, of which 3 were waited for; matrix products, arithmetic and copies ran while one was open for 4% of the time, Pallas kernels for 5%

profile of v5, /device:TPU:17, one launch (start us, length us, event | category | flops | bytes accessed | tf_op | source)
XLA Modules:
  0.0 55.6 jit_solution(425156146087129807)
XLA Ops:
  0.0 0.0 copy-start.1
  0.0 0.0 copy-start.2
  0.0 1.3 %broadcast_in_dim.10 = bf16[8,2,256]{2,1,0:T(2,128)(2,1)} broadcast(bf16[2,256]{1,0:T(2,128)(2,1)} %bitcast.128), dimensions={1,2} | broadcast | bytes 9216 | tf_op jit(solution)/shard_map/broadcast_in_dim | solution.py:118
  1.3 8.2 %all-to-all-start = ((bf16[8,2,256]{2,1,0:T(2,128)(2,1)}), bf16[8,2,256]{2,1,0:T(2,128)(2,1)S(1)}, u32[]{:S(2)}, u32[]{:S(2)}) async-start(bf16[8,2,256]{2,1,0:T(2,128)(2,1)} %broadcast_in_dim.10), calls=%async_computation | async-start | bytes 16384 | tf_op jit(solution)/shard_map/all_to_all | solution.py:117
  9.5 1.4 %copy.12 = bf16[256,1536]{0,1:T(8,128)(2,1)S(1)} copy(bf16[256,1536]{1,0:T(8,128)(2,1)} %param.8) | data formatting | bytes 1572864 | tf_op args[1]
  10.9 0.1 slice_bitcast_fusion
  11.0 0.0 copy-done.1
  11.0 0.0 copy-done.2
  11.0 5.0 %all-to-all-done = bf16[8,2,256]{2,1,0:T(2,128)(2,1)S(1)} async-done(((bf16[8,2,256]{2,1,0:T(2,128)(2,1)}), bf16[8,2,256]{2,1,0:T(2,128)(2,1)S(1)}, u32[]{:S(2)}, u32[]{:S(2)}) %all-to-all-start) | async-done | bytes 8224 | tf_op jit(solution)/shard_map/all_to_all | solution.py:117
  16.6 0.0 copy-start
  17.0 17.6 %all_to_all.10.recv_ref = bf16[16,120,256]{2,1,0:T(8,128)(2,1)S(1)} all-to-all(bf16[16,120,256]{2,1,0:T(8,128)(2,1)S(1)} %fusion.11), channel_id=1, replica_groups={{176,96,112,80,128,240,32,224,48,144,208,64,192,16,160,0},{184,104,120,..., dimensions={0} | all-to-all | bytes 1966080 | tf_op jit(solution)/shard_map/all_to_all | solution.py:142
  34.6 0.0 copy-done
  34.6 2.6 %shard_map.74 = f32[2,96,256]{2,1,0:T(8,128)S(1)} custom-call(bf16[128,256]{1,0:T(8,128)(2,1)S(1)} %copy-done, bf16[16,120,256]{2,1,0:T(8,128)(2,1)S(1)} %all_to_all.10.recv_ref), custom_call_target="tpu_custom_call" | custom-call | flops 805306368 | bytes 983040 | tf_op jit(solution)/shard_map/pallas_call | solution.py:97
  37.2 0.0 copy-start.3
  37.2 3.0 %collective-permute-start = (f32[2,96,256]{2,1,0:T(8,128)S(1)}, f32[2,96,256]{2,1,0:T(8,128)S(1)}, u32[]{:S(2)}, u32[]{:S(2)}) collective-permute-start(f32[2,96,256]{2,1,0:T(8,128)S(1)} %shard_map.74), channel_id=1, source_target_pairs={{0,8},{8,0},{16,24},{24,16},{32,40},{40,32},{48,56},{56,48},{64,72... | collective-permute-start | bytes 589832 | tf_op jit(solution)/shard_map/ppermute | solution.py:154
  40.2 2.6 %shard_map.73 = f32[2,96,256]{2,1,0:T(8,128)S(1)} custom-call(bf16[128,256]{1,0:T(8,128)(2,1)S(1)} %copy-done, bf16[16,120,256]{2,1,0:T(8,128)(2,1)S(1)} %all_to_all.10.recv_ref), custom_call_target="tpu_custom_call" | custom-call | flops 805306368 | bytes 983040 | tf_op jit(solution)/shard_map/pallas_call | solution.py:97
  42.8 0.0 collective-permute-done
  42.8 1.0 %collective-permute-start.1 = (f32[96,256]{1,0:T(8,128)S(1)}, f32[96,256]{1,0:T(8,128)S(1)}, u32[]{:S(2)}, u32[]{:S(2)}) collective-permute-start(f32[96,256]{1,0:T(8,128)S(1)} %get-tuple-element.9), channel_id=1, source_target_pairs={{0,2},{8,0},{16,18},{24,16},{32,34},{40,32},{48,50},{56,48},{2,70}... | collective-permute-start | bytes 294920 | tf_op jit(solution)/shard_map/ppermute | solution.py:169
  43.8 0.0 collective-permute-start.2
  43.8 0.0 copy-done.3
  43.8 0.6 %dynamic_slice.9 = s32[1]{0:T(128)} dynamic-slice(s32[8]{0:T(128)S(1)} %copy-done.3, s32[]{:T(128)S(6)} %select_n.70), dynamic_slice_sizes={1} | dynamic-slice | bytes 12 | tf_op jit(solution)/shard_map/dynamic_slice | solution.py:175
  45.1 8.3 %collective-permute-done.1 = f32[96,256]{1,0:T(8,128)S(1)} collective-permute-done((f32[96,256]{1,0:T(8,128)S(1)}, f32[96,256]{1,0:T(8,128)S(1)}, u32[]{:S(2)}, u32[]{:S(2)}) %collective-permute-start.1) | collective-permute-done | bytes 98336 | tf_op jit(solution)/shard_map/ppermute | solution.py:169
  53.4 0.1 copy.17
  53.5 0.9 %collective-permute-done.2 = f32[96,256]{1,0:T(8,128)S(1)} collective-permute-done((f32[96,256]{1,0:T(8,128)S(1)}, f32[96,256]{1,0:T(8,128)S(1)}, u32[]{:S(2)}, u32[]{:S(2)}) %collective-permute-start.2) | collective-permute-done | bytes 98336 | tf_op jit(solution)/shard_map/ppermute | solution.py:169
  54.4 0.1 copy.18
  54.5 0.2 fusion
  54.7 0.9 %copy.19 = f32[64,4,192]{2,1,0:T(4,128)} copy(f32[64,4,192]{2,0,1:T(8,128)S(1)} %fusion) | data formatting | bytes 393216 | tf_op jit(solution)/shard_map/transpose | solution.py:181
  (41 shorter events, 0.7 us)
Async XLA Ops:
  0.0 11.0 %copy-start.1 = (s32[256]{0:T(256)S(1)}, s32[256]{0:T(256)}, u32[]{:S(2)}) copy-start(s32[256]{0:T(256)} %param.10) | copy-start | bytes 3076
  0.0 11.0 %copy-start.2 = (s32[256]{0:T(256)S(1)}, s32[256]{0:T(256)}, u32[]{:S(2)}) copy-start(s32[256]{0:T(256)} %param.9) | copy-start | bytes 3076
  1.3 14.8 %all-to-all-start = ((bf16[8,2,256]{2,1,0:T(2,128)(2,1)}), bf16[8,2,256]{2,1,0:T(2,128)(2,1)S(1)}, u32[]{:S(2)}, u32[]{:S(2)}) async-start(bf16[8,2,256]{2,1,0:T(2,128)(2,1)} %broadcast_in_dim.10), calls=%async_computation | async-start | bytes 16384 | tf_op jit(solution)/shard_map/all_to_all | solution.py:117
  16.6 18.0 %copy-start = (bf16[128,256]{1,0:T(8,128)(2,1)S(1)}, bf16[128,256]{1,0:T(8,128)(2,1)}, u32[]{:S(2)}) copy-start(bf16[128,256]{1,0:T(8,128)(2,1)} %constant.59.clone.table_ref) | copy-start | bytes 196612
  37.2 6.6 %copy-start.3 = (s32[8]{0:T(128)S(1)}, s32[8]{0:T(128)}, u32[]{:S(2)}) copy-start(s32[8]{0:T(128)} %constant.60.clone) | copy-start | bytes 100
  37.2 5.6 %collective-permute-start = (f32[2,96,256]{2,1,0:T(8,128)S(1)}, f32[2,96,256]{2,1,0:T(8,128)S(1)}, u32[]{:S(2)}, u32[]{:S(2)}) collective-permute-start(f32[2,96,256]{2,1,0:T(8,128)S(1)} %shard_map.74), channel_id=1, source_target_pairs={{0,8},{8,0},{16,24},{24,16},{32,40},{40,32},{48,56},{56,48},{64,72... | collective-permute-start | bytes 589832 | tf_op jit(solution)/shard_map/ppermute | solution.py:154
  42.8 10.5 %collective-permute-start.1 = (f32[96,256]{1,0:T(8,128)S(1)}, f32[96,256]{1,0:T(8,128)S(1)}, u32[]{:S(2)}, u32[]{:S(2)}) collective-permute-start(f32[96,256]{1,0:T(8,128)S(1)} %get-tuple-element.9), channel_id=1, source_target_pairs={{0,2},{8,0},{16,18},{24,16},{32,34},{40,32},{48,50},{56,48},{2,70}... | collective-permute-start | bytes 294920 | tf_op jit(solution)/shard_map/ppermute | solution.py:169
  43.8 10.6 %collective-permute-start.2 = (f32[96,256]{1,0:T(8,128)S(1)}, f32[96,256]{1,0:T(8,128)S(1)}, u32[]{:S(2)}, u32[]{:S(2)}) collective-permute-start(f32[96,256]{1,0:T(8,128)S(1)} %get-tuple-element.10), channel_id=1, source_target_pairs={{0,6},{8,4},{16,22},{24,20},{32,38},{40,36},{48,54},{56,52},{2,68}... | collective-permute-start | bytes 294920 | tf_op jit(solution)/shard_map/ppermute | solution.py:169

commit v6 on v5

--- a/solution.py
+++ b/solution.py
@@ -17,12 +17,12 @@
 Z = 4
 CHIPS = Y * X
 COLS = 96
-META = GR + 8
+LANES = 128
 STEP = 4
 DISTANCE = (
     ((1, 3), (0, 2)),
-    ((0, 2), (1, 3)),
-    ((2, 1), (3, 0)),
+    ((0, 3), (2, 1)),
+    ((1, 0), (3, 2)),
     ((2, 1), (3, 0)),
 )
 HALVES = ((0, 3), (1, 2))
@@ -50,24 +50,32 @@
 
 
 def polarize(groups, table_ref, recv_ref, out_ref, sums_ref):
-    pairs = recv_ref.shape[2]
+    pairs = 2 * LANES
+
+    def both_halves(source, first, rows):
+        return jnp.concatenate(
+            [recv_ref[source, first + half * rows : first + (half + 1) * rows, :] for half in (0, 1)],
+            axis=1,
+        )
+
     bin_of_row = lax.broadcasted_iota(jnp.int32, (BINS, pairs), 0).astype(F32)
     for first in range(0, CHIPS, STEP):
         hots = []
         for source in range(first, first + STEP):
-            bins = recv_ref[source, COLS + GR : COLS + META, :].astype(F32)[0:1, :]
+            bins = recv_ref[source, 2 * (COLS + GR) :, :].astype(F32)
+            bins = jnp.concatenate([bins[0:1, :], bins[1:2, :]], axis=1)
             hots.append(jnp.where(bins == bin_of_row, 1.0, 0.0).astype(BF16))
         for place, group in enumerate(groups):
             total = None
             for source, hot in enumerate(hots, first):
-                slab = recv_ref[source, COLS : COLS + GR, :]
+                slab = both_halves(source, 2 * COLS, GR)
                 left = jnp.concatenate(
                     [hot * slab[row : row + 1, :] for row in range(4 * group, 4 * group + 4)],
                     axis=0,
                 )
                 term = lax.dot_general(
                     left,
-                    recv_ref[source, :COLS, :],
+                    both_halves(source, 0, COLS),
                     (((1,), (1,)), ((), ())),
                     preferred_element_type=F32,
                 )
@@ -100,7 +108,7 @@
         scratch_shapes=[pltpu.VMEM((rows, COLS), F32)],
         compiler_params=pltpu.CompilerParams(vmem_limit_bytes=40 * 1024 * 1024),
         cost_estimate=pl.CostEstimate(
-            flops=2 * rows * COLS * received.shape[0] * received.shape[2],
+            flops=2 * rows * COLS * received.shape[0] * 2 * LANES,
             bytes_accessed=2 * received.size,
             transcendentals=0,
         ),
@@ -123,24 +131,35 @@
     )
     slabs = slabs.reshape(Z, 4, pairs) * occupation[None, None, :].astype(BF16)
 
-    slabs = lax.dynamic_slice_in_dim(jnp.concatenate([slabs, slabs], axis=0), my_z, Z, 0)
-    bins = jnp.broadcast_to(bin_index.astype(BF16)[None, :], (META - GR, pairs))
+    codes = [0, 0]
+    for step in range(Y):
+        for c in range(CORES):
+            for place, group in enumerate(DISTANCE[step][c] + DISTANCE[step][1 - c]):
+                codes[c] |= group << (2 * (Z * step + place))
+    ys = sum(y << (2 * i) for i, (y, _) in enumerate(ORDER))
+    code = jnp.where(core == 0, np.uint32(codes[0]), np.uint32(codes[1]))
+    z = my_z.astype(jnp.uint32)
+    shape = (CHIPS, Z, 1, 1)
+    chip = lax.broadcasted_iota(jnp.uint32, shape, 0)
+    place = lax.broadcasted_iota(jnp.uint32, shape, 1)
+    step = ((np.uint32(ys) >> (2 * chip)) + Z - z) % Z
+    group = ((code >> (2 * (Z * step + place))) + z) % Z
+    meta = slabs[0]
+    for i in range(1, Z):
+        meta = jnp.where(group == i, slabs[i], meta)
+    meta = meta.reshape(CHIPS, GR, pairs)
+    meta = jnp.concatenate([meta[..., :LANES], meta[..., LANES:]], axis=1)
+    bins = jnp.pad(bin_index.astype(BF16).reshape(2, LANES), ((0, 6), (0, 0)))
+    bins = jnp.broadcast_to(bins[None], (CHIPS, 8, LANES))
+
     columns = column_density.T.reshape(X, Y, COLS, pairs)
-    payload = []
-    for step in range(Y):
-        keep, give = DISTANCE[step]
-        meta = jnp.where(
-            core == 0,
-            jnp.concatenate([slabs[i] for i in keep + give] + [bins], axis=0),
-            jnp.concatenate([slabs[i] for i in give + keep] + [bins], axis=0),
-        )
-        part = next(2 * c + HALVES[c].index(step) for c in range(CORES) if step in HALVES[c])
-        payload.append(
-            jnp.concatenate([columns[:, part], jnp.broadcast_to(meta[None], (X, META, pairs))], axis=1)
-        )
-    payload = lax.dynamic_slice_in_dim(jnp.stack(payload + payload), (Y - my_z) % Y, Y, 0)
+    columns = jnp.concatenate([columns[..., :LANES], columns[..., LANES:]], axis=2)
+    parts = [2 * c + HALVES[c].index(o) for o in range(Y) for c in range(CORES) if o in HALVES[c]]
+    columns = jnp.stack([columns[:, part] for part in parts + parts])
+    columns = lax.dynamic_slice_in_dim(columns, (Y - my_z) % Y, Y, 0)
+    columns = jnp.stack([columns[y, x] for y, x in ORDER])
     received = lax.all_to_all(
-        jnp.stack([payload[y, x] for y, x in ORDER]),
+        jnp.concatenate([columns, meta, bins], axis=1),
         "pair",
         0,
         0,
@@ -167,12 +186,12 @@
                         target = ((z * X + x) * CORES + to_core) * Z
                         moves.append((source, target + (z + DISTANCE[step][c][t]) % Z))
         arrived.append(lax.ppermute(summed[t], ("pair", "grow"), moves))
-    first = np.zeros((CORES, Z), np.int32)
+    first = 0
     for c in range(CORES):
-        for half in range(2):
-            for group in DISTANCE[HALVES[c][half]]:
-                first[c, group[0]] = half
-    my_first = jnp.asarray(first.reshape(-1))[core * Z + (my_z - my_y) % Z]
+        for half, step in enumerate(HALVES[c]):
+            for group in DISTANCE[step]:
+                first |= half << (Z * c + group[0])
+    my_first = (first >> (Z * core + (my_z - my_y) % Z)) & 1
     tiles = jnp.where(
         my_first == 0,
         jnp.concatenate(arrived, axis=0),

time: 56.2 us -> 54.5 us (0.970)
  waiting for transfers between devices: 14.3 us -> 8.77 us
  starting transfers between devices: 12.1 us -> 16.9 us
  between operations: 1.03 us -> 0.37 us
    ppermute x2, starting transfers between devices: 0.97 us -> 6.05 us  [per_device(): arrived.append(lax.ppermute(summed[t], ('pair', 'grow'), moves))]
    ppermute x2, waiting for transfers between devices: 9.25 us -> 5.02 us  [per_device(): arrived.append(lax.ppermute(summed[t], ('pair', 'grow'), moves))]
    all_to_all x1, waiting for transfers between devices: 5.03 us -> 3.74 us  [per_device(): lax.all_to_all(jnp.broadcast_to(slab_density.T[None], (GR // 2, 2, pairs)...]
    dynamic_slice x1 -> x0, local copies, waits for them, and re-layouts: 0.58 us -> none  [per_device(): my_first = jnp.asarray(first.reshape(-1))[core * Z + (my_z - my_y) % Z]]
    unnamed x24 -> x22, local copies, waits for them, and re-layouts: 1.65 us -> 1.89 us
  transfers between devices with their start and end apart: 4 -> 4, of which waited for: 3 -> 3; matrix products, arithmetic and copies ran while one was open for 4% -> 5% of each run, Pallas kernels for 5% -> 5%
where the time goes in v6:
time: 54.5 us; the launch traced here: 54.1 us
  blocking collectives  17.3 us (32%)
  starting transfers between devices  16.9 us (31%)
  waiting for transfers between devices  8.77 us (16%)
  Pallas kernels  5.2 us (10%)
  local copies, waits for them, and re-layouts  4.83 us (9%)
  other arithmetic  0.74 us (1%)
    all_to_all x1, blocking collectives, per_device(): lax.all_to_all(jnp.concatenate([columns, meta, bins], axis=1), 'pair', 0,...  17.3 us
    all_to_all x1, starting transfers between devices, per_device(): lax.all_to_all(jnp.broadcast_to(slab_density.T[None], (GR // 2, 2, pairs)...  8.19 us
    ppermute x2, starting transfers between devices, per_device(): arrived.append(lax.ppermute(summed[t], ('pair', 'grow'), moves))  6.05 us
    pallas_call x2, Pallas kernels, polarize_groups(): pl.pallas_call(functools.partial(polarize, groups), out_shape=jax.ShapeDt...  5.2 us
    ppermute x2, waiting for transfers between devices, per_device(): arrived.append(lax.ppermute(summed[t], ('pair', 'grow'), moves))  5.02 us
    all_to_all x1, waiting for transfers between devices, per_device(): lax.all_to_all(jnp.broadcast_to(slab_density.T[None], (GR // 2, 2, pairs)...  3.74 us
    ppermute x1, starting transfers between devices, per_device(): theirs = lax.ppermute(polarize_groups((2, 3), received), 'pair', swap)  2.68 us
    unnamed x22, local copies, waits for them, and re-layouts  1.89 us
  transfers between devices with their start and end apart: 4, of which 3 were waited for; matrix products, arithmetic and copies ran while one was open for 5% of the time, Pallas kernels for 5%

profile of v6, /device:TPU:17, one launch (start us, length us, event | category | flops | bytes accessed | tf_op | source)
XLA Modules:
  0.0 54.1 jit_solution(8305070365714322504)
XLA Ops:
  0.0 1.3 %broadcast_in_dim.87 = bf16[8,2,256]{2,1,0:T(2,128)(2,1)} broadcast(bf16[2,256]{1,0:T(2,128)(2,1)} %bitcast.130), dimensions={1,2} | broadcast | bytes 9216 | tf_op jit(solution)/shard_map/broadcast_in_dim | solution.py:126
  1.3 8.2 %all-to-all-start = ((bf16[8,2,256]{2,1,0:T(2,128)(2,1)}), bf16[8,2,256]{2,1,0:T(2,128)(2,1)S(1)}, u32[]{:S(2)}, u32[]{:S(2)}) async-start(bf16[8,2,256]{2,1,0:T(2,128)(2,1)} %broadcast_in_dim.87), calls=%async_computation | async-start | bytes 16384 | tf_op jit(solution)/shard_map/all_to_all | solution.py:125
  9.5 1.4 %copy.14 = bf16[256,1536]{0,1:T(8,128)(2,1)S(1)} copy(bf16[256,1536]{1,0:T(8,128)(2,1)} %param.9) | data formatting | bytes 1572864 | tf_op args[1]
  10.9 0.1 fusion.9
  11.1 0.1 constant_dynamic-update-slice_fusion.4
  11.3 0.0 copy-start.1
  11.3 0.0 copy-start.2
  11.8 0.2 copy-done.1
  12.0 0.1 copy.17
  12.1 0.1 copy.18
  12.2 0.1 copy.19
  12.3 0.0 copy-done.2
  12.3 3.7 %all-to-all-done = bf16[8,2,256]{2,1,0:T(2,128)(2,1)S(1)} async-done(((bf16[8,2,256]{2,1,0:T(2,128)(2,1)}), bf16[8,2,256]{2,1,0:T(2,128)(2,1)S(1)}, u32[]{:S(2)}, u32[]{:S(2)}) %all-to-all-start) | async-done | bytes 8224 | tf_op jit(solution)/shard_map/all_to_all | solution.py:125
  16.2 0.2 select_select_fusion
  16.4 0.0 copy-start
  16.4 0.1 pad_maximum_fusion
  16.5 17.3 %all_to_all.10.recv_ref = bf16[16,232,128]{2,1,0:T(8,128)(2,1)S(1)} all-to-all(bf16[16,232,128]{2,1,0:T(8,128)(2,1)S(1)} %pad_maximum_fusion), channel_id=1, replica_groups={{176,96,112,80,128,240,32,224,48,144,208,64,192,16,160,0},{184,104,120,..., dimensions={0} | all-to-all | bytes 1900544 | tf_op jit(solution)/shard_map/all_to_all | solution.py:161
  33.8 0.0 copy-done
  33.8 2.6 %shard_map.65 = f32[2,96,256]{2,1,0:T(8,128)S(1)} custom-call(bf16[128,256]{1,0:T(8,128)(2,1)S(1)} %copy-done, bf16[16,232,128]{2,1,0:T(8,128)(2,1)S(1)} %all_to_all.10.recv_ref), custom_call_target="tpu_custom_call" | custom-call | flops 805306368 | bytes 950272 | tf_op jit(solution)/shard_map/pallas_call | solution.py:105
  36.4 2.7 %collective-permute-start = (f32[2,96,256]{2,1,0:T(8,128)S(1)}, f32[2,96,256]{2,1,0:T(8,128)S(1)}, u32[]{:S(2)}, u32[]{:S(2)}) collective-permute-start(f32[2,96,256]{2,1,0:T(8,128)S(1)} %shard_map.65), channel_id=1, source_target_pairs={{0,8},{8,0},{16,24},{24,16},{32,40},{40,32},{48,56},{56,48},{64,72... | collective-permute-start | bytes 589832 | tf_op jit(solution)/shard_map/ppermute | solution.py:173
  39.1 2.6 %shard_map.64 = f32[2,96,256]{2,1,0:T(8,128)S(1)} custom-call(bf16[128,256]{1,0:T(8,128)(2,1)S(1)} %copy-done, bf16[16,232,128]{2,1,0:T(8,128)(2,1)S(1)} %all_to_all.10.recv_ref), custom_call_target="tpu_custom_call" | custom-call | flops 805306368 | bytes 950272 | tf_op jit(solution)/shard_map/pallas_call | solution.py:105
  41.7 0.0 collective-permute-done
  41.7 1.3 %collective-permute-start.1 = (f32[96,256]{1,0:T(8,128)S(1)}, f32[96,256]{1,0:T(8,128)S(1)}, u32[]{:S(2)}, u32[]{:S(2)}) collective-permute-start(f32[96,256]{1,0:T(8,128)S(1)} %get-tuple-element.10), channel_id=1, source_target_pairs={{0,2},{8,0},{16,18},{24,16},{32,34},{40,32},{48,50},{56,48},{2,70}... | collective-permute-start | bytes 294920 | tf_op jit(solution)/shard_map/ppermute | solution.py:188
  43.0 4.8 %collective-permute-start.2 = (f32[96,256]{1,0:T(8,128)S(1)}, f32[96,256]{1,0:T(8,128)S(1)}, u32[]{:S(2)}, u32[]{:S(2)}) collective-permute-start(f32[96,256]{1,0:T(8,128)S(1)} %get-tuple-element.11), channel_id=1, source_target_pairs={{0,6},{8,4},{16,22},{24,20},{32,38},{40,36},{48,54},{56,52},{2,68}... | collective-permute-start | bytes 294920 | tf_op jit(solution)/shard_map/ppermute | solution.py:188
  47.8 3.3 %collective-permute-done.1 = f32[96,256]{1,0:T(8,128)S(1)} collective-permute-done((f32[96,256]{1,0:T(8,128)S(1)}, f32[96,256]{1,0:T(8,128)S(1)}, u32[]{:S(2)}, u32[]{:S(2)}) %collective-permute-start.1) | collective-permute-done | bytes 98336 | tf_op jit(solution)/shard_map/ppermute | solution.py:188
  51.1 0.1 copy.20
  51.2 1.7 %collective-permute-done.2 = f32[96,256]{1,0:T(8,128)S(1)} collective-permute-done((f32[96,256]{1,0:T(8,128)S(1)}, f32[96,256]{1,0:T(8,128)S(1)}, u32[]{:S(2)}, u32[]{:S(2)}) %collective-permute-start.2) | collective-permute-done | bytes 98336 | tf_op jit(solution)/shard_map/ppermute | solution.py:188
  52.9 0.1 copy.21
  53.0 0.2 fusion
  53.2 0.9 %copy.22 = f32[64,4,192]{2,1,0:T(4,128)} copy(f32[64,4,192]{2,0,1:T(8,128)S(1)} %fusion) | data formatting | bytes 393216 | tf_op jit(solution)/shard_map/transpose | solution.py:200
  (46 shorter events, 0.7 us)
Async XLA Ops:
  1.3 14.8 %all-to-all-start = ((bf16[8,2,256]{2,1,0:T(2,128)(2,1)}), bf16[8,2,256]{2,1,0:T(2,128)(2,1)S(1)}, u32[]{:S(2)}, u32[]{:S(2)}) async-start(bf16[8,2,256]{2,1,0:T(2,128)(2,1)} %broadcast_in_dim.87), calls=%async_computation | async-start | bytes 16384 | tf_op jit(solution)/shard_map/all_to_all | solution.py:125
  11.3 0.7 %copy-start.1 = (s32[256]{0:T(256)S(1)}, s32[256]{0:T(256)}, u32[]{:S(2)}) copy-start(s32[256]{0:T(256)} %param.10) | copy-start | bytes 3076
  11.3 1.0 %copy-start.2 = (s32[256]{0:T(256)S(1)}, s32[256]{0:T(256)}, u32[]{:S(2)}) copy-start(s32[256]{0:T(256)} %param.11) | copy-start | bytes 3076
  16.4 17.4 %copy-start = (bf16[128,256]{1,0:T(8,128)(2,1)S(1)}, bf16[128,256]{1,0:T(8,128)(2,1)}, u32[]{:S(2)}) copy-start(bf16[128,256]{1,0:T(8,128)(2,1)} %constant.82.clone.table_ref) | copy-start | bytes 196612
  36.4 5.3 %collective-permute-start = (f32[2,96,256]{2,1,0:T(8,128)S(1)}, f32[2,96,256]{2,1,0:T(8,128)S(1)}, u32[]{:S(2)}, u32[]{:S(2)}) collective-permute-start(f32[2,96,256]{2,1,0:T(8,128)S(1)} %shard_map.65), channel_id=1, source_target_pairs={{0,8},{8,0},{16,24},{24,16},{32,40},{40,32},{48,56},{56,48},{64,72... | collective-permute-start | bytes 589832 | tf_op jit(solution)/shard_map/ppermute | solution.py:173
  41.7 9.3 %collective-permute-start.1 = (f32[96,256]{1,0:T(8,128)S(1)}, f32[96,256]{1,0:T(8,128)S(1)}, u32[]{:S(2)}, u32[]{:S(2)}) collective-permute-start(f32[96,256]{1,0:T(8,128)S(1)} %get-tuple-element.10), channel_id=1, source_target_pairs={{0,2},{8,0},{16,18},{24,16},{32,34},{40,32},{48,50},{56,48},{2,70}... | collective-permute-start | bytes 294920 | tf_op jit(solution)/shard_map/ppermute | solution.py:188
  43.0 9.9 %collective-permute-start.2 = (f32[96,256]{1,0:T(8,128)S(1)}, f32[96,256]{1,0:T(8,128)S(1)}, u32[]{:S(2)}, u32[]{:S(2)}) collective-permute-start(f32[96,256]{1,0:T(8,128)S(1)} %get-tuple-element.11), channel_id=1, source_target_pairs={{0,6},{8,4},{16,22},{24,20},{32,38},{40,36},{48,54},{56,52},{2,68}... | collective-permute-start | bytes 294920 | tf_op jit(solution)/shard_map/ppermute | solution.py:188

commit v7 on v6

--- a/solution.py
+++ b/solution.py
@@ -26,7 +26,7 @@
     ((2, 1), (3, 0)),
 )
 HALVES = ((0, 3), (1, 2))
-ORDER = ((2, 3), (1, 2), (1, 3), (1, 1), (2, 0), (3, 3), (0, 2), (3, 2), (0, 3), (2, 1), (3, 1), (1, 0), (3, 0), (0, 1), (2, 2), (0, 0))
+ORDER = ((2, 2), (3, 3), (0, 2), (3, 2), (0, 1), (2, 1), (1, 3), (2, 3), (1, 1), (3, 0), (2, 0), (3, 1), (0, 3), (1, 0), (0, 0), (1, 2))
 BF16 = jnp.bfloat16
 F32 = jnp.float32
 
@@ -49,7 +49,7 @@
     return np.block([[high, high], [low, low]])
 
 
-def polarize(groups, table_ref, recv_ref, out_ref, sums_ref):
+def polarize(groups, table_ref, bins_ref, recv_ref, out_ref, sums_ref):
     pairs = 2 * LANES
 
     def both_halves(source, first, rows):
@@ -62,8 +62,7 @@
     for first in range(0, CHIPS, STEP):
         hots = []
         for source in range(first, first + STEP):
-            bins = recv_ref[source, 2 * (COLS + GR) :, :].astype(F32)
-            bins = jnp.concatenate([bins[0:1, :], bins[1:2, :]], axis=1)
+            bins = bins_ref[source : source + 1, :]
             hots.append(jnp.where(bins == bin_of_row, 1.0, 0.0).astype(BF16))
         for place, group in enumerate(groups):
             total = None
@@ -100,7 +99,7 @@
         out_ref[duo // 2, :, lane : lane + 2 * FREQS] = jnp.concatenate(both, axis=0).T
 
 
-def polarize_groups(groups, received):
+def polarize_groups(groups, bins, received):
     rows = len(groups) * 4 * BINS
     return pl.pallas_call(
         functools.partial(polarize, groups),
@@ -112,7 +111,7 @@
             bytes_accessed=2 * received.size,
             transcendentals=0,
         ),
-    )(jnp.asarray(split_table()), received)
+    )(jnp.asarray(split_table()), bins, received)
 
 
 def per_device(slab_density, column_density, bin_index, occupation):
@@ -169,9 +168,11 @@
         tiled=True,
     )
 
+    bins = received[:, 2 * (COLS + GR) :][:, :2].reshape(CHIPS, pairs).astype(F32)
+    received = received[:, : 2 * (COLS + GR)]
     swap = [(i, i ^ 1) for i in range(Y * X * CORES)]
-    theirs = lax.ppermute(polarize_groups((2, 3), received), "pair", swap)
-    summed = polarize_groups((0, 1), received) + theirs
+    theirs = lax.ppermute(polarize_groups((2, 3), bins, received), "pair", swap)
+    summed = polarize_groups((0, 1), bins, received) + theirs
 
     arrived = []
     for t in range(2):

time: 54.5 us -> 54.4 us (level)
  blocking collectives: 17.3 us -> 15.5 us
  starting transfers between devices: 16.9 us -> 18.2 us
    all_to_all x1, blocking collectives: 17.3 us -> 15.5 us  [per_device(): lax.all_to_all(jnp.concatenate([columns, meta, bins], axis=1), 'pair', 0,...]
    ppermute x1, starting transfers between devices: 2.68 us -> 3.97 us  [per_device(): theirs = lax.ppermute(polarize_groups((2, 3), bins, received), 'pair', swap)]
    unnamed x22 -> x23, local copies, waits for them, and re-layouts: 1.89 us -> 1.89 us
where the time goes in v7:
time: 54.4 us; the launch traced here: 54.1 us
  starting transfers between devices  18.2 us (33%)
  blocking collectives  15.5 us (28%)
  waiting for transfers between devices  9.13 us (17%)
  Pallas kernels  5.19 us (10%)
  local copies, waits for them, and re-layouts  4.9 us (9%)
  other arithmetic  0.75 us (1%)
    all_to_all x1, blocking collectives, per_device(): lax.all_to_all(jnp.concatenate([columns, meta, bins], axis=1), 'pair', 0,...  15.5 us
    all_to_all x1, starting transfers between devices, per_device(): lax.all_to_all(jnp.broadcast_to(slab_density.T[None], (GR // 2, 2, pairs)...  8.19 us
    ppermute x2, starting transfers between devices, per_device(): arrived.append(lax.ppermute(summed[t], ('pair', 'grow'), moves))  6.05 us
    ppermute x2, waiting for transfers between devices, per_device(): arrived.append(lax.ppermute(summed[t], ('pair', 'grow'), moves))  5.38 us
    pallas_call x2, Pallas kernels, polarize_groups(): pl.pallas_call(functools.partial(polarize, groups), out_shape=jax.ShapeDt...  5.19 us
    ppermute x1, starting transfers between devices, per_device(): theirs = lax.ppermute(polarize_groups((2, 3), bins, received), 'pair', swap)  3.97 us
    all_to_all x1, waiting for transfers between devices, per_device(): lax.all_to_all(jnp.broadcast_to(slab_density.T[None], (GR // 2, 2, pairs)...  3.74 us
    unnamed x23, local copies, waits for them, and re-layouts  1.89 us
  transfers between devices with their start and end apart: 4, of which 3 were waited for; matrix products, arithmetic and copies ran while one was open for 5% of the time, Pallas kernels for 5%

profile of v7, /device:TPU:17, one launch (start us, length us, event | category | flops | bytes accessed | tf_op | source)
XLA Modules:
  0.0 54.1 jit_solution(2392993825903275173)
XLA Ops:
  0.0 1.3 %broadcast_in_dim.87 = bf16[8,2,256]{2,1,0:T(2,128)(2,1)} broadcast(bf16[2,256]{1,0:T(2,128)(2,1)} %bitcast.137), dimensions={1,2} | broadcast | bytes 9216 | tf_op jit(solution)/shard_map/broadcast_in_dim | solution.py:125
  1.3 8.2 %all-to-all-start = ((bf16[8,2,256]{2,1,0:T(2,128)(2,1)}), bf16[8,2,256]{2,1,0:T(2,128)(2,1)S(1)}, u32[]{:S(2)}, u32[]{:S(2)}) async-start(bf16[8,2,256]{2,1,0:T(2,128)(2,1)} %broadcast_in_dim.87), calls=%async_computation | async-start | bytes 16384 | tf_op jit(solution)/shard_map/all_to_all | solution.py:124
  9.5 1.4 %copy.14 = bf16[256,1536]{0,1:T(8,128)(2,1)S(1)} copy(bf16[256,1536]{1,0:T(8,128)(2,1)} %param.9) | data formatting | bytes 1572864 | tf_op args[1]
  10.9 0.1 fusion.9
  11.1 0.1 constant_dynamic-update-slice_fusion.4
  11.3 0.0 copy-start.1
  11.3 0.0 copy-start.2
  11.8 0.2 copy-done.1
  12.0 0.1 copy.17
  12.1 0.1 copy.18
  12.2 0.1 copy.19
  12.3 0.0 copy-done.2
  12.3 3.7 %all-to-all-done = bf16[8,2,256]{2,1,0:T(2,128)(2,1)S(1)} async-done(((bf16[8,2,256]{2,1,0:T(2,128)(2,1)}), bf16[8,2,256]{2,1,0:T(2,128)(2,1)S(1)}, u32[]{:S(2)}, u32[]{:S(2)}) %all-to-all-start) | async-done | bytes 8224 | tf_op jit(solution)/shard_map/all_to_all | solution.py:124
  16.2 0.2 select_select_fusion
  16.4 0.1 pad_maximum_fusion
  16.5 0.0 copy-start
  16.5 15.5 %all_to_all.10 = bf16[16,232,128]{2,1,0:T(8,128)(2,1)S(1)} all-to-all(bf16[16,232,128]{2,1,0:T(8,128)(2,1)S(1)} %pad_maximum_fusion), channel_id=1, replica_groups={{160,240,32,224,16,144,112,176,80,192,128,208,48,64,0,96},{168,248,40,2..., dimensions={0} | all-to-all | bytes 1900544 | tf_op jit(solution)/shard_map/all_to_all | solution.py:160
  32.0 0.1 slice.149.recv_ref
  32.1 0.0 copy-done
  32.1 2.6 %shard_map.65 = f32[2,96,256]{2,1,0:T(8,128)S(1)} custom-call(bf16[128,256]{1,0:T(8,128)(2,1)S(1)} %copy-done, f32[16,256]{1,0:T(8,128)S(1)} %bitcast.128, bf16[16,224,128]{2,1,0:T(8,128)(2,1)S(1)} %slice.149.recv_ref), custom_call_target="tpu_custom_call" | custom-call | flops 805306368 | bytes 917504 | tf_op jit(solution)/shard_map/pallas_call | solution.py:104
  34.7 4.0 %collective-permute-start = (f32[2,96,256]{2,1,0:T(8,128)S(1)}, f32[2,96,256]{2,1,0:T(8,128)S(1)}, u32[]{:S(2)}, u32[]{:S(2)}) collective-permute-start(f32[2,96,256]{2,1,0:T(8,128)S(1)} %shard_map.65), channel_id=1, source_target_pairs={{0,8},{8,0},{16,24},{24,16},{32,40},{40,32},{48,56},{56,48},{64,72... | collective-permute-start | bytes 589832 | tf_op jit(solution)/shard_map/ppermute | solution.py:174
  38.7 2.6 %shard_map.64 = f32[2,96,256]{2,1,0:T(8,128)S(1)} custom-call(bf16[128,256]{1,0:T(8,128)(2,1)S(1)} %copy-done, f32[16,256]{1,0:T(8,128)S(1)} %bitcast.129, bf16[16,224,128]{2,1,0:T(8,128)(2,1)S(1)} %slice.149.recv_ref), custom_call_target="tpu_custom_call" | custom-call | flops 805306368 | bytes 917504 | tf_op jit(solution)/shard_map/pallas_call | solution.py:104
  41.3 0.0 collective-permute-done
  41.3 1.6 %collective-permute-start.1 = (f32[96,256]{1,0:T(8,128)S(1)}, f32[96,256]{1,0:T(8,128)S(1)}, u32[]{:S(2)}, u32[]{:S(2)}) collective-permute-start(f32[96,256]{1,0:T(8,128)S(1)} %get-tuple-element.10), channel_id=1, source_target_pairs={{0,2},{8,0},{16,18},{24,16},{32,34},{40,32},{48,50},{56,48},{2,70}... | collective-permute-start | bytes 294920 | tf_op jit(solution)/shard_map/ppermute | solution.py:189
  43.0 4.4 %collective-permute-start.2 = (f32[96,256]{1,0:T(8,128)S(1)}, f32[96,256]{1,0:T(8,128)S(1)}, u32[]{:S(2)}, u32[]{:S(2)}) collective-permute-start(f32[96,256]{1,0:T(8,128)S(1)} %get-tuple-element.11), channel_id=1, source_target_pairs={{0,6},{8,4},{16,22},{24,20},{32,38},{40,36},{48,54},{56,52},{2,68}... | collective-permute-start | bytes 294920 | tf_op jit(solution)/shard_map/ppermute | solution.py:189
  47.4 3.4 %collective-permute-done.1 = f32[96,256]{1,0:T(8,128)S(1)} collective-permute-done((f32[96,256]{1,0:T(8,128)S(1)}, f32[96,256]{1,0:T(8,128)S(1)}, u32[]{:S(2)}, u32[]{:S(2)}) %collective-permute-start.1) | collective-permute-done | bytes 98336 | tf_op jit(solution)/shard_map/ppermute | solution.py:189
  50.8 0.1 copy.20
  50.9 2.0 %collective-permute-done.2 = f32[96,256]{1,0:T(8,128)S(1)} collective-permute-done((f32[96,256]{1,0:T(8,128)S(1)}, f32[96,256]{1,0:T(8,128)S(1)}, u32[]{:S(2)}, u32[]{:S(2)}) %collective-permute-start.2) | collective-permute-done | bytes 98336 | tf_op jit(solution)/shard_map/ppermute | solution.py:189
  52.9 0.1 copy.21
  53.0 0.2 fusion
  53.2 0.9 %copy.22 = f32[64,4,192]{2,1,0:T(4,128)} copy(f32[64,4,192]{2,0,1:T(8,128)S(1)} %fusion) | data formatting | bytes 393216 | tf_op jit(solution)/shard_map/transpose | solution.py:201
  (48 shorter events, 0.7 us)
Async XLA Ops:
  1.3 14.8 %all-to-all-start = ((bf16[8,2,256]{2,1,0:T(2,128)(2,1)}), bf16[8,2,256]{2,1,0:T(2,128)(2,1)S(1)}, u32[]{:S(2)}, u32[]{:S(2)}) async-start(bf16[8,2,256]{2,1,0:T(2,128)(2,1)} %broadcast_in_dim.87), calls=%async_computation | async-start | bytes 16384 | tf_op jit(solution)/shard_map/all_to_all | solution.py:124
  11.3 0.7 %copy-start.1 = (s32[256]{0:T(256)S(1)}, s32[256]{0:T(256)}, u32[]{:S(2)}) copy-start(s32[256]{0:T(256)} %param.10) | copy-start | bytes 3076
  11.3 1.0 %copy-start.2 = (s32[256]{0:T(256)S(1)}, s32[256]{0:T(256)}, u32[]{:S(2)}) copy-start(s32[256]{0:T(256)} %param.11) | copy-start | bytes 3076
  16.5 15.6 %copy-start = (bf16[128,256]{1,0:T(8,128)(2,1)S(1)}, bf16[128,256]{1,0:T(8,128)(2,1)}, u32[]{:S(2)}) copy-start(bf16[128,256]{1,0:T(8,128)(2,1)} %constant.82.clone.table_ref) | copy-start | bytes 196612
  34.7 6.6 %collective-permute-start = (f32[2,96,256]{2,1,0:T(8,128)S(1)}, f32[2,96,256]{2,1,0:T(8,128)S(1)}, u32[]{:S(2)}, u32[]{:S(2)}) collective-permute-start(f32[2,96,256]{2,1,0:T(8,128)S(1)} %shard_map.65), channel_id=1, source_target_pairs={{0,8},{8,0},{16,24},{24,16},{32,40},{40,32},{48,56},{56,48},{64,72... | collective-permute-start | bytes 589832 | tf_op jit(solution)/shard_map/ppermute | solution.py:174
  41.3 9.5 %collective-permute-start.1 = (f32[96,256]{1,0:T(8,128)S(1)}, f32[96,256]{1,0:T(8,128)S(1)}, u32[]{:S(2)}, u32[]{:S(2)}) collective-permute-start(f32[96,256]{1,0:T(8,128)S(1)} %get-tuple-element.10), channel_id=1, source_target_pairs={{0,2},{8,0},{16,18},{24,16},{32,34},{40,32},{48,50},{56,48},{2,70}... | collective-permute-start | bytes 294920 | tf_op jit(solution)/shard_map/ppermute | solution.py:189
  43.0 9.9 %collective-permute-start.2 = (f32[96,256]{1,0:T(8,128)S(1)}, f32[96,256]{1,0:T(8,128)S(1)}, u32[]{:S(2)}, u32[]{:S(2)}) collective-permute-start(f32[96,256]{1,0:T(8,128)S(1)} %get-tuple-element.11), channel_id=1, source_target_pairs={{0,6},{8,4},{16,22},{24,20},{32,38},{40,36},{48,54},{56,52},{2,68}... | collective-permute-start | bytes 294920 | tf_op jit(solution)/shard_map/ppermute | solution.py:189

commit v8 on v7

--- a/solution.py
+++ b/solution.py
@@ -169,7 +169,6 @@
     )
 
     bins = received[:, 2 * (COLS + GR) :][:, :2].reshape(CHIPS, pairs).astype(F32)
-    received = received[:, : 2 * (COLS + GR)]
     swap = [(i, i ^ 1) for i in range(Y * X * CORES)]
     theirs = lax.ppermute(polarize_groups((2, 3), bins, received), "pair", swap)
     summed = polarize_groups((0, 1), bins, received) + theirs

time: 54.4 us -> 54.2 us (level)
  no operation moved by 1% of the time
where the time goes in v8:
time: 54.2 us; the launch traced here: 53.9 us
  starting transfers between devices  18.2 us (34%)
  blocking collectives  15.4 us (28%)
  waiting for transfers between devices  9.12 us (17%)
  Pallas kernels  5.19 us (10%)
  local copies, waits for them, and re-layouts  4.84 us (9%)
  other arithmetic  0.74 us (1%)
    all_to_all x1, blocking collectives, per_device(): lax.all_to_all(jnp.concatenate([columns, meta, bins], axis=1), 'pair', 0,...  15.4 us
    all_to_all x1, starting transfers between devices, per_device(): lax.all_to_all(jnp.broadcast_to(slab_density.T[None], (GR // 2, 2, pairs)...  8.19 us
    ppermute x2, starting transfers between devices, per_device(): arrived.append(lax.ppermute(summed[t], ('pair', 'grow'), moves))  6.06 us
    ppermute x2, waiting for transfers between devices, per_device(): arrived.append(lax.ppermute(summed[t], ('pair', 'grow'), moves))  5.38 us
    pallas_call x2, Pallas kernels, polarize_groups(): pl.pallas_call(functools.partial(polarize, groups), out_shape=jax.ShapeDt...  5.19 us
    ppermute x1, starting transfers between devices, per_device(): theirs = lax.ppermute(polarize_groups((2, 3), bins, received), 'pair', swap)  3.98 us
    all_to_all x1, waiting for transfers between devices, per_device(): lax.all_to_all(jnp.broadcast_to(slab_density.T[None], (GR // 2, 2, pairs)...  3.74 us
    unnamed x23, local copies, waits for them, and re-layouts  1.89 us
  transfers between devices with their start and end apart: 4, of which 3 were waited for; matrix products, arithmetic and copies ran while one was open for 5% of the time, Pallas kernels for 5%

profile of v8, /device:TPU:17, one launch (start us, length us, event | category | flops | bytes accessed | tf_op | source)
XLA Modules:
  0.0 53.9 jit_solution(8497467043452110019)
XLA Ops:
  0.0 1.3 %broadcast_in_dim.87 = bf16[8,2,256]{2,1,0:T(2,128)(2,1)} broadcast(bf16[2,256]{1,0:T(2,128)(2,1)} %bitcast.137), dimensions={1,2} | broadcast | bytes 9216 | tf_op jit(solution)/shard_map/broadcast_in_dim | solution.py:125
  1.3 8.2 %all-to-all-start = ((bf16[8,2,256]{2,1,0:T(2,128)(2,1)}), bf16[8,2,256]{2,1,0:T(2,128)(2,1)S(1)}, u32[]{:S(2)}, u32[]{:S(2)}) async-start(bf16[8,2,256]{2,1,0:T(2,128)(2,1)} %broadcast_in_dim.87), calls=%async_computation | async-start | bytes 16384 | tf_op jit(solution)/shard_map/all_to_all | solution.py:124
  9.5 1.4 %copy.14 = bf16[256,1536]{0,1:T(8,128)(2,1)S(1)} copy(bf16[256,1536]{1,0:T(8,128)(2,1)} %param.9) | data formatting | bytes 1572864 | tf_op args[1]
  10.9 0.1 fusion.9
  11.1 0.1 constant_dynamic-update-slice_fusion.4
  11.3 0.0 copy-start.1
  11.3 0.0 copy-start.2
  11.8 0.2 copy-done.1
  12.0 0.1 copy.17
  12.1 0.1 copy.18
  12.2 0.1 copy.19
  12.3 0.0 copy-done.2
  12.3 3.7 %all-to-all-done = bf16[8,2,256]{2,1,0:T(2,128)(2,1)S(1)} async-done(((bf16[8,2,256]{2,1,0:T(2,128)(2,1)}), bf16[8,2,256]{2,1,0:T(2,128)(2,1)S(1)}, u32[]{:S(2)}, u32[]{:S(2)}) %all-to-all-start) | async-done | bytes 8224 | tf_op jit(solution)/shard_map/all_to_all | solution.py:124
  16.2 0.2 select_select_fusion
  16.4 0.0 copy-start
  16.4 0.1 pad_maximum_fusion
  16.5 15.4 %all_to_all.10.recv_ref = bf16[16,232,128]{2,1,0:T(8,128)(2,1)S(1)} all-to-all(bf16[16,232,128]{2,1,0:T(8,128)(2,1)S(1)} %pad_maximum_fusion), channel_id=1, replica_groups={{160,240,32,224,16,144,112,176,80,192,128,208,48,64,0,96},{168,248,40,2..., dimensions={0} | all-to-all | bytes 1900544 | tf_op jit(solution)/shard_map/all_to_all | solution.py:160
  31.9 0.0 copy-done
  31.9 2.6 %shard_map.65 = f32[2,96,256]{2,1,0:T(8,128)S(1)} custom-call(bf16[128,256]{1,0:T(8,128)(2,1)S(1)} %copy-done, f32[16,256]{1,0:T(8,128)S(1)} %bitcast.128, bf16[16,232,128]{2,1,0:T(8,128)(2,1)S(1)} %all_to_all.10.recv_ref), custom_call_target="tpu_custom_call" | custom-call | flops 805306368 | bytes 950272 | tf_op jit(solution)/shard_map/pallas_call | solution.py:104
  34.5 4.0 %collective-permute-start = (f32[2,96,256]{2,1,0:T(8,128)S(1)}, f32[2,96,256]{2,1,0:T(8,128)S(1)}, u32[]{:S(2)}, u32[]{:S(2)}) collective-permute-start(f32[2,96,256]{2,1,0:T(8,128)S(1)} %shard_map.65), channel_id=1, source_target_pairs={{0,8},{8,0},{16,24},{24,16},{32,40},{40,32},{48,56},{56,48},{64,72... | collective-permute-start | bytes 589832 | tf_op jit(solution)/shard_map/ppermute | solution.py:173
  38.5 2.6 %shard_map.64 = f32[2,96,256]{2,1,0:T(8,128)S(1)} custom-call(bf16[128,256]{1,0:T(8,128)(2,1)S(1)} %copy-done, f32[16,256]{1,0:T(8,128)S(1)} %bitcast.129, bf16[16,232,128]{2,1,0:T(8,128)(2,1)S(1)} %all_to_all.10.recv_ref), custom_call_target="tpu_custom_call" | custom-call | flops 805306368 | bytes 950272 | tf_op jit(solution)/shard_map/pallas_call | solution.py:104
  41.1 0.0 collective-permute-done
  41.1 1.6 %collective-permute-start.1 = (f32[96,256]{1,0:T(8,128)S(1)}, f32[96,256]{1,0:T(8,128)S(1)}, u32[]{:S(2)}, u32[]{:S(2)}) collective-permute-start(f32[96,256]{1,0:T(8,128)S(1)} %get-tuple-element.10), channel_id=1, source_target_pairs={{0,2},{8,0},{16,18},{24,16},{32,34},{40,32},{48,50},{56,48},{2,70}... | collective-permute-start | bytes 294920 | tf_op jit(solution)/shard_map/ppermute | solution.py:188
  42.7 4.5 %collective-permute-start.2 = (f32[96,256]{1,0:T(8,128)S(1)}, f32[96,256]{1,0:T(8,128)S(1)}, u32[]{:S(2)}, u32[]{:S(2)}) collective-permute-start(f32[96,256]{1,0:T(8,128)S(1)} %get-tuple-element.11), channel_id=1, source_target_pairs={{0,6},{8,4},{16,22},{24,20},{32,38},{40,36},{48,54},{56,52},{2,68}... | collective-permute-start | bytes 294920 | tf_op jit(solution)/shard_map/ppermute | solution.py:188
  47.2 3.4 %collective-permute-done.1 = f32[96,256]{1,0:T(8,128)S(1)} collective-permute-done((f32[96,256]{1,0:T(8,128)S(1)}, f32[96,256]{1,0:T(8,128)S(1)}, u32[]{:S(2)}, u32[]{:S(2)}) %collective-permute-start.1) | collective-permute-done | bytes 98336 | tf_op jit(solution)/shard_map/ppermute | solution.py:188
  50.6 0.1 copy.20
  50.7 2.0 %collective-permute-done.2 = f32[96,256]{1,0:T(8,128)S(1)} collective-permute-done((f32[96,256]{1,0:T(8,128)S(1)}, f32[96,256]{1,0:T(8,128)S(1)}, u32[]{:S(2)}, u32[]{:S(2)}) %collective-permute-start.2) | collective-permute-done | bytes 98336 | tf_op jit(solution)/shard_map/ppermute | solution.py:188
  52.7 0.1 copy.21
  52.8 0.2 fusion
  53.0 0.9 %copy.22 = f32[64,4,192]{2,1,0:T(4,128)} copy(f32[64,4,192]{2,0,1:T(8,128)S(1)} %fusion) | data formatting | bytes 393216 | tf_op jit(solution)/shard_map/transpose | solution.py:200
  (48 shorter events, 0.7 us)
Async XLA Ops:
  1.3 14.8 %all-to-all-start = ((bf16[8,2,256]{2,1,0:T(2,128)(2,1)}), bf16[8,2,256]{2,1,0:T(2,128)(2,1)S(1)}, u32[]{:S(2)}, u32[]{:S(2)}) async-start(bf16[8,2,256]{2,1,0:T(2,128)(2,1)} %broadcast_in_dim.87), calls=%async_computation | async-start | bytes 16384 | tf_op jit(solution)/shard_map/all_to_all | solution.py:124
  11.3 0.7 %copy-start.1 = (s32[256]{0:T(256)S(1)}, s32[256]{0:T(256)}, u32[]{:S(2)}) copy-start(s32[256]{0:T(256)} %param.10) | copy-start | bytes 3076
  11.3 1.0 %copy-start.2 = (s32[256]{0:T(256)S(1)}, s32[256]{0:T(256)}, u32[]{:S(2)}) copy-start(s32[256]{0:T(256)} %param.11) | copy-start | bytes 3076
  16.4 15.5 %copy-start = (bf16[128,256]{1,0:T(8,128)(2,1)S(1)}, bf16[128,256]{1,0:T(8,128)(2,1)}, u32[]{:S(2)}) copy-start(bf16[128,256]{1,0:T(8,128)(2,1)} %constant.82.clone.table_ref) | copy-start | bytes 196612
  34.5 6.6 %collective-permute-start = (f32[2,96,256]{2,1,0:T(8,128)S(1)}, f32[2,96,256]{2,1,0:T(8,128)S(1)}, u32[]{:S(2)}, u32[]{:S(2)}) collective-permute-start(f32[2,96,256]{2,1,0:T(8,128)S(1)} %shard_map.65), channel_id=1, source_target_pairs={{0,8},{8,0},{16,24},{24,16},{32,40},{40,32},{48,56},{56,48},{64,72... | collective-permute-start | bytes 589832 | tf_op jit(solution)/shard_map/ppermute | solution.py:173
  41.1 9.5 %collective-permute-start.1 = (f32[96,256]{1,0:T(8,128)S(1)}, f32[96,256]{1,0:T(8,128)S(1)}, u32[]{:S(2)}, u32[]{:S(2)}) collective-permute-start(f32[96,256]{1,0:T(8,128)S(1)} %get-tuple-element.10), channel_id=1, source_target_pairs={{0,2},{8,0},{16,18},{24,16},{32,34},{40,32},{48,50},{56,48},{2,70}... | collective-permute-start | bytes 294920 | tf_op jit(solution)/shard_map/ppermute | solution.py:188
  42.7 9.9 %collective-permute-start.2 = (f32[96,256]{1,0:T(8,128)S(1)}, f32[96,256]{1,0:T(8,128)S(1)}, u32[]{:S(2)}, u32[]{:S(2)}) collective-permute-start(f32[96,256]{1,0:T(8,128)S(1)} %get-tuple-element.11), channel_id=1, source_target_pairs={{0,6},{8,4},{16,22},{24,20},{32,38},{40,36},{48,54},{56,52},{2,68}... | collective-permute-start | bytes 294920 | tf_op jit(solution)/shard_map/ppermute | solution.py:188
